TPU v7x, 32 devices: a whole 2x2x4 slice. The times are simulated.
32 devices in a mesh: band: 4 (over x, core), col: 8 (over z, y).
Axes of the slice: x: 2, y: 2, z: 4, core: 2. Of those that a mesh axis runs over, the one named last changes fastest.
Arguments:
- left_image: bfloat16 [16, 1024, 256], P('band', 'col'), may hold values from -6 to 6
- right_image: bfloat16 [16, 1024, 256], P('band', 'col'), may hold values from -6 to 6
- kernel: bfloat16 [2304, 256], replicated, may hold values from -0.125 to 0.125
- valid_mask: int32 [16, 1024], P('band', 'col'), may hold values 0 or 1
- disparity: int32 [16, 1024], P('band', 'col'), may hold values from 0 to 511
Outputs:
- grad_left: bfloat16 [16, 1024, 256], P('band', 'col')
- grad_right: bfloat16 [16, 1024, 256], P('band', 'col')
All inputs are finite; a program needn't handle non-finite values. No bound on the sum of `valid_mask` on one device may be relied on, other than what follows from the above.
Results may differ from a plain program's by a relative error of at most 0.011.
Values may be sent and summed in bfloat16 or wider, within the bound.
A program may use at most 64 MiB of HBM per device.

v0:
```python
import jax
import jax.numpy as jnp
from jax import lax
from jax.sharding import PartitionSpec as P

DISP = 512


def extended(block, sides, width):
    for axis, dim in sides:
        count = lax.axis_size(axis)
        forward = [(i, i + 1) for i in range(count - 1)]
        backward = [(target, source) for source, target in forward]
        low = lax.ppermute(
            lax.slice_in_dim(block, block.shape[dim] - width, None, axis=dim), axis, forward
        )
        high = lax.ppermute(lax.slice_in_dim(block, 0, width, axis=dim), axis, backward)
        block = jnp.concatenate([low, block, high], axis=dim)
    return block


def passed_along(value, axis, steps):
    count = lax.axis_size(axis)
    leading, last = (max(0, -steps), min(count, count - steps))
    return lax.ppermute(value, axis, [(source, source + steps) for source in range(leading, last)])


def conv_pair(padded, weights):
    pairs = padded.shape[0]
    height = padded.shape[1] - 2
    columns = padded.shape[2] - 2
    channels = padded.shape[3]
    pieces = [
        padded[:, row_off : row_off + height, col_off : col_off + columns]
        for row_off in range(3)
        for col_off in range(3)
    ]
    patches = jnp.concatenate(pieces, axis=3).reshape(pairs * height * columns, 9 * channels)
    result = jnp.dot(patches, weights, preferred_element_type=jnp.float32)
    return result.reshape(pairs, height, columns, weights.shape[1])


def band_to_diagonals(scores, reach):
    height, columns, extent = scores.shape
    flattened = scores.reshape(height, columns * extent)
    flattened = jnp.concatenate([flattened, jnp.zeros((height, columns), scores.dtype)], 1)
    return flattened.reshape(height, columns, extent + 1)[:, :, 1 : reach + 1]


def diagonals_to_band(reversed_rows, reach):
    height, columns, _ = reversed_rows.shape
    extent = columns + reach
    widened = jnp.concatenate(
        [
            jnp.zeros((height, columns, 1), reversed_rows.dtype),
            reversed_rows,
            jnp.zeros((height, columns, columns), reversed_rows.dtype),
        ],
        2,
    )
    flattened = widened.reshape(height, columns * (extent + 1))[:, : columns * extent]
    return flattened.reshape(height, columns, extent)


def shards(left_image, right_image, kernel, valid_mask, disparity):
    columns = left_image.shape[1]
    channels = left_image.shape[2]
    reach_devs = DISP // columns
    factor = channels ** (-0.5)
    stacked = jnp.stack((left_image, right_image), 0)
    rimmed = extended(stacked, (("band", 1), ("col", 2)), 1)
    features = conv_pair(rimmed, kernel).astype(jnp.bfloat16)
    left_feat = features[0]
    right_feat = features[1]
    received = [
        passed_along(right_feat, "col", reach_devs - position) for position in range(reach_devs)
    ]
    segment = jnp.concatenate(received + [right_feat], 1)
    scores = (
        jnp.einsum("rxc,ryc->rxy", left_feat, segment, preferred_element_type=jnp.float32) * factor
    )
    correlation = band_to_diagonals(scores, DISP)[:, :, ::-1]
    disparities = jnp.arange(DISP, dtype=jnp.int32)
    distance = (disparities[None, None, :] - disparity[:, :, None]).astype(jnp.float32)
    target = jnp.exp(-distance * distance / 8.0)
    validity = valid_mask.astype(jnp.float32)[:, :, None]
    gradient = (validity * (correlation - target) * (channels / DISP)).astype(jnp.bfloat16)
    banded = diagonals_to_band(gradient[:, :, ::-1], DISP)
    left_term = (
        jnp.einsum("rxy,ryc->rxc", banded, segment, preferred_element_type=jnp.float32) * factor
    )
    segment_term = (
        jnp.einsum("rxy,rxc->ryc", banded, left_feat, preferred_element_type=jnp.float32) * factor
    )
    pieces = [
        segment_term[:, position * columns : (position + 1) * columns]
        for position in range(reach_devs)
    ]
    own_part = segment_term[:, reach_devs * columns :]
    summed = own_part
    for position in range(reach_devs):
        summed = summed + passed_along(
            pieces[position].astype(jnp.bfloat16), "col", position - reach_devs
        ).astype(jnp.float32)
    grads = jnp.stack((left_term.astype(jnp.bfloat16), summed.astype(jnp.bfloat16)), 0)
    grad_padded = extended(grads, (("band", 1), ("col", 2)), 1)
    blocks = kernel.reshape(3, 3, channels, channels)[::-1, ::-1]
    flipped = jnp.transpose(blocks, (0, 1, 3, 2)).reshape(9 * channels, channels)
    outputs = conv_pair(grad_padded, flipped).astype(jnp.bfloat16)
    return (outputs[0], outputs[1])


def solution(mesh):
    return jax.shard_map(
        shards,
        mesh=mesh,
        in_specs=(
            P("band", "col", None),
            P("band", "col", None),
            P(),
            P("band", "col"),
            P("band", "col"),
        ),
        out_specs=(P("band", "col", None), P("band", "col", None)),
        check_vma=False,
    )
```

profile of v0, /device:TPU:1, one launch (start us, length us, event | category | flops | bytes accessed | tf_op | source)
XLA Modules:
  0.0 130.4 jit_solution(3318704515840928944)
XLA Ops:
  0.7 1.0 fusion.27
  1.7 4.5 %collective-permute-start = (bf16[2,1,128,256]{3,2,1,0:T(8,128)(2,1)S(1)}, bf16[2,1,128,256]{3,2,1,0:T(8,128)(2,1)S(1)}, u32[]{:S(2)}, u32[]{:S(2)}) collective-permute-start(bf16[2,1,128,256]{3,2,1,0:T(8,128)(2,1)S(1)} %get-tuple-element.18), channel_id=1, source_target_pairs={{0,8},{8,16},{16,24},{1,9},{9,17},{17,25},{2,10},{10,18},{18,26},{... | collective-permute-start | bytes 393224 | tf_op jit(solution)/shard_map/ppermute | solution.py:14
  6.2 1.9 %collective-permute-start.1 = (bf16[2,1,128,256]{3,2,1,0:T(8,128)(2,1)S(1)}, bf16[2,1,128,256]{3,2,1,0:T(8,128)(2,1)S(1)}, u32[]{:S(2)}, u32[]{:S(2)}) collective-permute-start(bf16[2,1,128,256]{3,2,1,0:T(8,128)(2,1)S(1)} %get-tuple-element.19), channel_id=1, source_target_pairs={{8,0},{16,8},{24,16},{9,1},{17,9},{25,17},{10,2},{18,10},{26,18},{... | collective-permute-start | bytes 393224 | tf_op jit(solution)/shard_map/ppermute | solution.py:17
  8.1 4.3 %collective-permute-done.1 = bf16[2,1,128,256]{3,2,1,0:T(8,128)(2,1)S(1)} collective-permute-done((bf16[2,1,128,256]{3,2,1,0:T(8,128)(2,1)S(1)}, bf16[2,1,128,256]{3,2,1,0:T(8,128)(2,1)S(1)}, u32[]{:S(2)}, u32[]{:S(2)}) %collective-permute-start.1) | collective-permute-done | bytes 131104 | tf_op jit(solution)/shard_map/ppermute | solution.py:17
  12.5 0.8 pad_maximum_fusion.16
  13.3 3.1 %collective-permute-start.2 = (bf16[2,6,1,256]{3,2,1,0:T(2,128)(2,1)S(1)}, bf16[2,6,1,256]{3,2,1,0:T(2,128)(2,1)S(1)}, u32[]{:S(2)}, u32[]{:S(2)}) collective-permute-start(bf16[2,6,1,256]{3,2,1,0:T(2,128)(2,1)S(1)} %get-tuple-element.13), channel_id=1, source_target_pairs={{0,1},{1,2},{2,3},{3,4},{4,5},{5,6},{6,7},{8,9},{9,10},{10,11},{11... | collective-permute-start | bytes 18440 | tf_op jit(solution)/shard_map/ppermute | solution.py:14
  16.4 1.3 collective-permute-start.3
  17.7 3.1 %collective-permute-done.3 = bf16[2,6,1,256]{3,2,1,0:T(2,128)(2,1)S(1)} collective-permute-done((bf16[2,6,1,256]{3,2,1,0:T(2,128)(2,1)S(1)}, bf16[2,6,1,256]{3,2,1,0:T(2,128)(2,1)S(1)}, u32[]{:S(2)}, u32[]{:S(2)}) %collective-permute-start.3) | collective-permute-done | bytes 6176 | tf_op jit(solution)/shard_map/ppermute | solution.py:17
  20.9 0.3 pad_maximum_fusion
  21.9 1.0 copy-done.4
  22.9 1.4 %convolution_convert_fusion.1 = bf16[2,4,128,256]{3,2,1,0:T(8,128)(2,1)S(1)} fusion(bf16[2,4,128,2304]{3,2,1,0:T(8,128)(2,1)S(1)} %slice_dynamic-update-slice_fusion.6, bf16[2304,256]{1,0:T(8,128)(2,1)S(1)} %copy-done.4), kind=kOutput, calls=%fused_computation.5 | convolution fusion | flops 1208221696 | bytes 6422528 | tf_op jit(solution)/shard_map/dot_general | solution.py:39
  24.4 4.2 %collective-permute-start.4 = (bf16[4,128,256]{2,1,0:T(8,128)(2,1)S(1)}, bf16[4,128,256]{2,1,0:T(8,128)(2,1)S(1)}, u32[]{:S(2)}, u32[]{:S(2)}) collective-permute-start(bf16[4,128,256]{2,1,0:T(8,128)(2,1)S(1)} %slice_bitcast_fusion.2), channel_id=1, source_target_pairs={{0,4},{1,5},{2,6},{3,7},{8,12},{9,13},{10,14},{11,15},{16,20},{17,... | collective-permute-start | bytes 786440 | tf_op jit(solution)/shard_map/ppermute | solution.py:25
  28.6 2.7 %collective-permute-start.5 = (bf16[4,128,256]{2,1,0:T(8,128)(2,1)S(1)}, bf16[4,128,256]{2,1,0:T(8,128)(2,1)S(1)}, u32[]{:S(2)}, u32[]{:S(2)}) collective-permute-start(bf16[4,128,256]{2,1,0:T(8,128)(2,1)S(1)} %slice_bitcast_fusion.2), channel_id=1, source_target_pairs={{0,3},{1,4},{2,5},{3,6},{4,7},{8,11},{9,12},{10,13},{11,14},{12,15... | collective-permute-start | bytes 786440 | tf_op jit(solution)/shard_map/ppermute | solution.py:25
  31.3 2.7 %collective-permute-start.6 = (bf16[4,128,256]{2,1,0:T(8,128)(2,1)S(1)}, bf16[4,128,256]{2,1,0:T(8,128)(2,1)S(1)}, u32[]{:S(2)}, u32[]{:S(2)}) collective-permute-start(bf16[4,128,256]{2,1,0:T(8,128)(2,1)S(1)} %slice_bitcast_fusion.2), channel_id=1, source_target_pairs={{0,2},{1,3},{2,4},{3,5},{4,6},{5,7},{8,10},{9,11},{10,12},{11,13},... | collective-permute-start | bytes 786440 | tf_op jit(solution)/shard_map/ppermute | solution.py:25
  34.1 2.2 %collective-permute-start.7 = (bf16[4,128,256]{2,1,0:T(8,128)(2,1)S(1)}, bf16[4,128,256]{2,1,0:T(8,128)(2,1)S(1)}, u32[]{:S(2)}, u32[]{:S(2)}) collective-permute-start(bf16[4,128,256]{2,1,0:T(8,128)(2,1)S(1)} %slice_bitcast_fusion.2), channel_id=1, source_target_pairs={{0,1},{1,2},{2,3},{3,4},{4,5},{5,6},{6,7},{8,9},{9,10},{10,11},{11... | collective-permute-start | bytes 786440 | tf_op jit(solution)/shard_map/ppermute | solution.py:25
  36.4 4.0 %collective-permute-done.5 = bf16[4,128,256]{2,1,0:T(8,128)(2,1)S(1)} collective-permute-done((bf16[4,128,256]{2,1,0:T(8,128)(2,1)S(1)}, bf16[4,128,256]{2,1,0:T(8,128)(2,1)S(1)}, u32[]{:S(2)}, u32[]{:S(2)}) %collective-permute-start.5) | collective-permute-done | bytes 262176 | tf_op jit(solution)/shard_map/ppermute | solution.py:25
  40.4 4.4 %collective-permute-done.6 = bf16[4,128,256]{2,1,0:T(8,128)(2,1)S(1)} collective-permute-done((bf16[4,128,256]{2,1,0:T(8,128)(2,1)S(1)}, bf16[4,128,256]{2,1,0:T(8,128)(2,1)S(1)}, u32[]{:S(2)}, u32[]{:S(2)}) %collective-permute-start.6) | collective-permute-done | bytes 262176 | tf_op jit(solution)/shard_map/ppermute | solution.py:25
  45.0 1.1 copy-done.2
  46.0 0.5 fusion
  46.6 0.8 copy.14
  47.4 0.2 concatenate.62
  47.7 1.6 %reshape.33 = f32[4,128,641]{2,1,0:T(8,128)S(1)} reshape(f32[4,82048]{1,0:T(4,128)S(1)} %concatenate.62) | data formatting | bytes 2625536 | tf_op jit(solution)/shard_map/reshape | solution.py:47
  49.3 0.3 slice.172
  49.6 1.5 %rev.9 = f32[4,128,512]{2,1,0:T(8,128)S(1)} reverse(f32[4,128,512]{2,1,0:T(8,128)S(1)} %slice.172), dimensions={2} | reverse | bytes 2097152 | tf_op jit(solution)/shard_map/rev | solution.py:82
  51.1 0.4 fusion.9
  51.6 1.6 %rev.10 = bf16[4,128,512]{2,1,0:T(8,128)(2,1)S(1)} reverse(bf16[4,128,512]{2,1,0:T(8,128)(2,1)S(1)} %fusion.9), dimensions={2} | reverse | bytes 1048576 | tf_op jit(solution)/shard_map/rev | solution.py:88
  53.3 0.4 maximum_maximum_fusion.2
  53.6 1.6 %reshape.34 = bf16[4,82048]{1,0:T(4,128)(2,1)S(1)} reshape(bf16[4,128,641]{2,1,0:T(8,128)(2,1)S(1)} %maximum_maximum_fusion.2) | data formatting | bytes 1312768 | tf_op jit(solution)/shard_map/reshape | solution.py:61
  55.2 0.2 slice.173
  55.5 0.6 fusion.30
  56.1 1.4 %collective-permute-start.10 = (bf16[4,128,256]{2,1,0:T(8,128)(2,1)S(1)}, bf16[4,128,256]{2,1,0:T(8,128)(2,1)S(1)}, u32[]{:S(2)}, u32[]{:S(2)}) collective-permute-start(bf16[4,128,256]{2,1,0:T(8,128)(2,1)S(1)} %get-tuple-element.4), channel_id=1, source_target_pairs={{2,0},{3,1},{4,2},{5,3},{6,4},{7,5},{10,8},{11,9},{12,10},{13,11},... | collective-permute-start | bytes 786440 | tf_op jit(solution)/shard_map/ppermute | solution.py:25
  57.6 1.3 collective-permute-start.11
  58.9 1.3 collective-permute-start.8
  60.2 1.3 collective-permute-start.9
  61.5 0.4 fusion.3
  61.9 12.2 %collective-permute-done.10 = bf16[4,128,256]{2,1,0:T(8,128)(2,1)S(1)} collective-permute-done((bf16[4,128,256]{2,1,0:T(8,128)(2,1)S(1)}, bf16[4,128,256]{2,1,0:T(8,128)(2,1)S(1)}, u32[]{:S(2)}, u32[]{:S(2)}) %collective-permute-start.10) | collective-permute-done | bytes 262176 | tf_op jit(solution)/shard_map/ppermute | solution.py:25
  74.0 32.0 %collective-permute-done.8 = bf16[4,128,256]{2,1,0:T(8,128)(2,1)S(1)} collective-permute-done((bf16[4,128,256]{2,1,0:T(8,128)(2,1)S(1)}, bf16[4,128,256]{2,1,0:T(8,128)(2,1)S(1)}, u32[]{:S(2)}, u32[]{:S(2)}) %collective-permute-start.8) | collective-permute-done | bytes 262176 | tf_op jit(solution)/shard_map/ppermute | solution.py:25
  106.0 0.2 fusion.24
  106.2 2.1 %collective-permute-start.12 = (bf16[2,1,128,256]{3,2,1,0:T(8,128)(2,1)S(1)}, bf16[2,1,128,256]{3,2,1,0:T(8,128)(2,1)S(1)}, u32[]{:S(2)}, u32[]{:S(2)}) collective-permute-start(bf16[2,1,128,256]{3,2,1,0:T(8,128)(2,1)S(1)} %get-tuple-element.16), channel_id=1, source_target_pairs={{0,8},{8,16},{16,24},{1,9},{9,17},{17,25},{2,10},{10,18},{18,26},{... | collective-permute-start | bytes 393224 | tf_op jit(solution)/shard_map/ppermute | solution.py:14
  108.3 2.4 %collective-permute-start.13 = (bf16[2,1,128,256]{3,2,1,0:T(8,128)(2,1)S(1)}, bf16[2,1,128,256]{3,2,1,0:T(8,128)(2,1)S(1)}, u32[]{:S(2)}, u32[]{:S(2)}) collective-permute-start(bf16[2,1,128,256]{3,2,1,0:T(8,128)(2,1)S(1)} %get-tuple-element.17), channel_id=1, source_target_pairs={{8,0},{16,8},{24,16},{9,1},{17,9},{25,17},{10,2},{18,10},{26,18},{... | collective-permute-start | bytes 393224 | tf_op jit(solution)/shard_map/ppermute | solution.py:17
  110.7 3.9 %collective-permute-done.13 = bf16[2,1,128,256]{3,2,1,0:T(8,128)(2,1)S(1)} collective-permute-done((bf16[2,1,128,256]{3,2,1,0:T(8,128)(2,1)S(1)}, bf16[2,1,128,256]{3,2,1,0:T(8,128)(2,1)S(1)}, u32[]{:S(2)}, u32[]{:S(2)}) %collective-permute-start.13) | collective-permute-done | bytes 131104 | tf_op jit(solution)/shard_map/ppermute | solution.py:17
  114.6 8.1 %collective-permute-start.14 = (bf16[2,6,1,256]{3,2,1,0:T(2,128)(2,1)S(1)}, bf16[2,6,1,256]{3,2,1,0:T(2,128)(2,1)S(1)}, u32[]{:S(2)}, u32[]{:S(2)}) collective-permute-start(bf16[2,6,1,256]{3,2,1,0:T(2,128)(2,1)S(1)} %get-tuple-element.9), channel_id=1, source_target_pairs={{0,1},{1,2},{2,3},{3,4},{4,5},{5,6},{6,7},{8,9},{9,10},{10,11},{11... | collective-permute-start | bytes 18440 | tf_op jit(solution)/shard_map/ppermute | solution.py:14
  122.7 1.5 %collective-permute-start.15 = (bf16[2,6,1,256]{3,2,1,0:T(2,128)(2,1)S(1)}, bf16[2,6,1,256]{3,2,1,0:T(2,128)(2,1)S(1)}, u32[]{:S(2)}, u32[]{:S(2)}) collective-permute-start(bf16[2,6,1,256]{3,2,1,0:T(2,128)(2,1)S(1)} %get-tuple-element.8), channel_id=1, source_target_pairs={{1,0},{2,1},{3,2},{4,3},{5,4},{6,5},{7,6},{9,8},{10,9},{11,10},{12... | collective-permute-start | bytes 18440 | tf_op jit(solution)/shard_map/ppermute | solution.py:17
  124.3 0.7 copy.10
  125.1 2.1 %collective-permute-done.15 = bf16[2,6,1,256]{3,2,1,0:T(2,128)(2,1)S(1)} collective-permute-done((bf16[2,6,1,256]{3,2,1,0:T(2,128)(2,1)S(1)}, bf16[2,6,1,256]{3,2,1,0:T(2,128)(2,1)S(1)}, u32[]{:S(2)}, u32[]{:S(2)}) %collective-permute-start.15) | collective-permute-done | bytes 6176 | tf_op jit(solution)/shard_map/ppermute | solution.py:17
  127.2 0.3 pad_maximum_fusion.1
  128.2 1.4 %convolution_convert_fusion = bf16[2,4,128,256]{3,2,1,0:T(8,128)(2,1)S(1)} fusion(bf16[2,4,128,2304]{3,2,1,0:T(8,128)(2,1)S(1)} %slice_dynamic-update-slice_fusion, bf16[2304,256,1,1]{1,0,3,2:T(8,128)(2,1)S(1)} %bitcast.66), kind=kOutput, calls=%fused_computation.4 | convolution fusion | flops 1208221696 | bytes 6422528 | tf_op jit(solution)/shard_map/dot_general | solution.py:39
  129.6 0.8 slice_bitcast_fusion
  (54 shorter events, 1.7 us)
Async XLA Ops:
  0.6 20.2 %copy-start = (bf16[4,128,256]{2,1,0:T(8,128)(2,1)S(1)}, bf16[4,128,256]{2,1,0:T(8,128)(2,1)}, u32[]{:S(2)}) copy-start(bf16[4,128,256]{2,1,0:T(8,128)(2,1)} %param.5) | copy-start | bytes 786436
  0.6 20.2 %copy-start.1 = (bf16[4,128,256]{2,1,0:T(8,128)(2,1)S(1)}, bf16[4,128,256]{2,1,0:T(8,128)(2,1)}, u32[]{:S(2)}) copy-start(bf16[4,128,256]{2,1,0:T(8,128)(2,1)} %param.6) | copy-start | bytes 786436
  1.7 6.4 %collective-permute-start = (bf16[2,1,128,256]{3,2,1,0:T(8,128)(2,1)S(1)}, bf16[2,1,128,256]{3,2,1,0:T(8,128)(2,1)S(1)}, u32[]{:S(2)}, u32[]{:S(2)}) collective-permute-start(bf16[2,1,128,256]{3,2,1,0:T(8,128)(2,1)S(1)} %get-tuple-element.18), channel_id=1, source_target_pairs={{0,8},{8,16},{16,24},{1,9},{9,17},{17,25},{2,10},{10,18},{18,26},{... | collective-permute-start | bytes 393224 | tf_op jit(solution)/shard_map/ppermute | solution.py:14
  6.2 6.3 %collective-permute-start.1 = (bf16[2,1,128,256]{3,2,1,0:T(8,128)(2,1)S(1)}, bf16[2,1,128,256]{3,2,1,0:T(8,128)(2,1)S(1)}, u32[]{:S(2)}, u32[]{:S(2)}) collective-permute-start(bf16[2,1,128,256]{3,2,1,0:T(8,128)(2,1)S(1)} %get-tuple-element.19), channel_id=1, source_target_pairs={{8,0},{16,8},{24,16},{9,1},{17,9},{25,17},{10,2},{18,10},{26,18},{... | collective-permute-start | bytes 393224 | tf_op jit(solution)/shard_map/ppermute | solution.py:17
  13.3 4.5 %collective-permute-start.2 = (bf16[2,6,1,256]{3,2,1,0:T(2,128)(2,1)S(1)}, bf16[2,6,1,256]{3,2,1,0:T(2,128)(2,1)S(1)}, u32[]{:S(2)}, u32[]{:S(2)}) collective-permute-start(bf16[2,6,1,256]{3,2,1,0:T(2,128)(2,1)S(1)} %get-tuple-element.13), channel_id=1, source_target_pairs={{0,1},{1,2},{2,3},{3,4},{4,5},{5,6},{6,7},{8,9},{9,10},{10,11},{11... | collective-permute-start | bytes 18440 | tf_op jit(solution)/shard_map/ppermute | solution.py:14
  16.4 4.4 %collective-permute-start.3 = (bf16[2,6,1,256]{3,2,1,0:T(2,128)(2,1)S(1)}, bf16[2,6,1,256]{3,2,1,0:T(2,128)(2,1)S(1)}, u32[]{:S(2)}, u32[]{:S(2)}) collective-permute-start(bf16[2,6,1,256]{3,2,1,0:T(2,128)(2,1)S(1)} %get-tuple-element.12), channel_id=1, source_target_pairs={{1,0},{2,1},{3,2},{4,3},{5,4},{6,5},{7,6},{9,8},{10,9},{11,10},{12... | collective-permute-start | bytes 18440 | tf_op jit(solution)/shard_map/ppermute | solution.py:17
  21.7 1.3 copy-start.4
  22.9 11.0 %copy-start.7 = (s32[4,128]{1,0:T(4,128)S(1)}, s32[4,128]{1,0:T(4,128)}, u32[]{:S(2)}) copy-start(s32[4,128]{1,0:T(4,128)} %param.8) | copy-start | bytes 6148
  24.4 12.0 %collective-permute-start.4 = (bf16[4,128,256]{2,1,0:T(8,128)(2,1)S(1)}, bf16[4,128,256]{2,1,0:T(8,128)(2,1)S(1)}, u32[]{:S(2)}, u32[]{:S(2)}) collective-permute-start(bf16[4,128,256]{2,1,0:T(8,128)(2,1)S(1)} %slice_bitcast_fusion.2), channel_id=1, source_target_pairs={{0,4},{1,5},{2,6},{3,7},{8,12},{9,13},{10,14},{11,15},{16,20},{17,... | collective-permute-start | bytes 786440 | tf_op jit(solution)/shard_map/ppermute | solution.py:25
  28.6 11.8 %collective-permute-start.5 = (bf16[4,128,256]{2,1,0:T(8,128)(2,1)S(1)}, bf16[4,128,256]{2,1,0:T(8,128)(2,1)S(1)}, u32[]{:S(2)}, u32[]{:S(2)}) collective-permute-start(bf16[4,128,256]{2,1,0:T(8,128)(2,1)S(1)} %slice_bitcast_fusion.2), channel_id=1, source_target_pairs={{0,3},{1,4},{2,5},{3,6},{4,7},{8,11},{9,12},{10,13},{11,14},{12,15... | collective-permute-start | bytes 786440 | tf_op jit(solution)/shard_map/ppermute | solution.py:25
  31.3 13.6 %collective-permute-start.6 = (bf16[4,128,256]{2,1,0:T(8,128)(2,1)S(1)}, bf16[4,128,256]{2,1,0:T(8,128)(2,1)S(1)}, u32[]{:S(2)}, u32[]{:S(2)}) collective-permute-start(bf16[4,128,256]{2,1,0:T(8,128)(2,1)S(1)} %slice_bitcast_fusion.2), channel_id=1, source_target_pairs={{0,2},{1,3},{2,4},{3,5},{4,6},{5,7},{8,10},{9,11},{10,12},{11,13},... | collective-permute-start | bytes 786440 | tf_op jit(solution)/shard_map/ppermute | solution.py:25
  34.1 10.8 %collective-permute-start.7 = (bf16[4,128,256]{2,1,0:T(8,128)(2,1)S(1)}, bf16[4,128,256]{2,1,0:T(8,128)(2,1)S(1)}, u32[]{:S(2)}, u32[]{:S(2)}) collective-permute-start(bf16[4,128,256]{2,1,0:T(8,128)(2,1)S(1)} %slice_bitcast_fusion.2), channel_id=1, source_target_pairs={{0,1},{1,2},{2,3},{3,4},{4,5},{5,6},{6,7},{8,9},{9,10},{10,11},{11... | collective-permute-start | bytes 786440 | tf_op jit(solution)/shard_map/ppermute | solution.py:25
  45.0 1.1 copy-start.2
  49.3 1.8 %copy-start.6 = (s32[4,128]{1,0:T(4,128)S(1)}, s32[4,128]{1,0:T(4,128)}, u32[]{:S(2)}) copy-start(s32[4,128]{1,0:T(4,128)} %param.9) | copy-start | bytes 6148
  56.0 5.4 %copy-start.3 = (bf16[4,640,256]{2,1,0:T(8,128)(2,1)S(1)}, bf16[4,640,256]{2,1,0:T(8,128)(2,1)}, u32[]{:S(2)}) copy-start(bf16[4,640,256]{2,1,0:T(8,128)(2,1)} %copy-done.2) | copy-start | bytes 3932164
  56.1 17.9 %collective-permute-start.10 = (bf16[4,128,256]{2,1,0:T(8,128)(2,1)S(1)}, bf16[4,128,256]{2,1,0:T(8,128)(2,1)S(1)}, u32[]{:S(2)}, u32[]{:S(2)}) collective-permute-start(bf16[4,128,256]{2,1,0:T(8,128)(2,1)S(1)} %get-tuple-element.4), channel_id=1, source_target_pairs={{2,0},{3,1},{4,2},{5,3},{6,4},{7,5},{10,8},{11,9},{12,10},{13,11},... | collective-permute-start | bytes 786440 | tf_op jit(solution)/shard_map/ppermute | solution.py:25
  57.6 16.5 %collective-permute-start.11 = (bf16[4,128,256]{2,1,0:T(8,128)(2,1)S(1)}, bf16[4,128,256]{2,1,0:T(8,128)(2,1)S(1)}, u32[]{:S(2)}, u32[]{:S(2)}) collective-permute-start(bf16[4,128,256]{2,1,0:T(8,128)(2,1)S(1)} %get-tuple-element.3), channel_id=1, source_target_pairs={{1,0},{2,1},{3,2},{4,3},{5,4},{6,5},{7,6},{9,8},{10,9},{11,10},{12... | collective-permute-start | bytes 786440 | tf_op jit(solution)/shard_map/ppermute | solution.py:25
  58.9 47.1 %collective-permute-start.8 = (bf16[4,128,256]{2,1,0:T(8,128)(2,1)S(1)}, bf16[4,128,256]{2,1,0:T(8,128)(2,1)S(1)}, u32[]{:S(2)}, u32[]{:S(2)}) collective-permute-start(bf16[4,128,256]{2,1,0:T(8,128)(2,1)S(1)} %get-tuple-element.2), channel_id=1, source_target_pairs={{4,0},{5,1},{6,2},{7,3},{12,8},{13,9},{14,10},{15,11},{20,16},{21,... | collective-permute-start | bytes 786440 | tf_op jit(solution)/shard_map/ppermute | solution.py:25
  60.2 45.8 %collective-permute-start.9 = (bf16[4,128,256]{2,1,0:T(8,128)(2,1)S(1)}, bf16[4,128,256]{2,1,0:T(8,128)(2,1)S(1)}, u32[]{:S(2)}, u32[]{:S(2)}) collective-permute-start(bf16[4,128,256]{2,1,0:T(8,128)(2,1)S(1)} %get-tuple-element.5), channel_id=1, source_target_pairs={{3,0},{4,1},{5,2},{6,3},{7,4},{11,8},{12,9},{13,10},{14,11},{15,12... | collective-permute-start | bytes 786440 | tf_op jit(solution)/shard_map/ppermute | solution.py:25
  106.0 18.2 %copy-start.5 = (bf16[2304,256]{1,0:T(8,128)(2,1)S(1)}, bf16[2304,256]{1,0:T(8,128)(2,1)}, u32[]{:S(2)}) copy-start(bf16[2304,256]{1,0:T(8,128)(2,1)} %param.7) | copy-start | bytes 3538948
  106.2 4.5 %collective-permute-start.12 = (bf16[2,1,128,256]{3,2,1,0:T(8,128)(2,1)S(1)}, bf16[2,1,128,256]{3,2,1,0:T(8,128)(2,1)S(1)}, u32[]{:S(2)}, u32[]{:S(2)}) collective-permute-start(bf16[2,1,128,256]{3,2,1,0:T(8,128)(2,1)S(1)} %get-tuple-element.16), channel_id=1, source_target_pairs={{0,8},{8,16},{16,24},{1,9},{9,17},{17,25},{2,10},{10,18},{18,26},{... | collective-permute-start | bytes 393224 | tf_op jit(solution)/shard_map/ppermute | solution.py:14
  108.3 6.3 %collective-permute-start.13 = (bf16[2,1,128,256]{3,2,1,0:T(8,128)(2,1)S(1)}, bf16[2,1,128,256]{3,2,1,0:T(8,128)(2,1)S(1)}, u32[]{:S(2)}, u32[]{:S(2)}) collective-permute-start(bf16[2,1,128,256]{3,2,1,0:T(8,128)(2,1)S(1)} %get-tuple-element.17), channel_id=1, source_target_pairs={{8,0},{16,8},{24,16},{9,1},{17,9},{25,17},{10,2},{18,10},{26,18},{... | collective-permute-start | bytes 393224 | tf_op jit(solution)/shard_map/ppermute | solution.py:17
  114.6 10.5 %collective-permute-start.14 = (bf16[2,6,1,256]{3,2,1,0:T(2,128)(2,1)S(1)}, bf16[2,6,1,256]{3,2,1,0:T(2,128)(2,1)S(1)}, u32[]{:S(2)}, u32[]{:S(2)}) collective-permute-start(bf16[2,6,1,256]{3,2,1,0:T(2,128)(2,1)S(1)} %get-tuple-element.9), channel_id=1, source_target_pairs={{0,1},{1,2},{2,3},{3,4},{4,5},{5,6},{6,7},{8,9},{9,10},{10,11},{11... | collective-permute-start | bytes 18440 | tf_op jit(solution)/shard_map/ppermute | solution.py:14
  122.7 4.4 %collective-permute-start.15 = (bf16[2,6,1,256]{3,2,1,0:T(2,128)(2,1)S(1)}, bf16[2,6,1,256]{3,2,1,0:T(2,128)(2,1)S(1)}, u32[]{:S(2)}, u32[]{:S(2)}) collective-permute-start(bf16[2,6,1,256]{3,2,1,0:T(2,128)(2,1)S(1)} %get-tuple-element.8), channel_id=1, source_target_pairs={{1,0},{2,1},{3,2},{4,3},{5,4},{6,5},{7,6},{9,8},{10,9},{11,10},{12... | collective-permute-start | bytes 18440 | tf_op jit(solution)/shard_map/ppermute | solution.py:17
where the time goes:
time: 131 us; the launch traced here: 130 us
  waiting for transfers between devices  66.1 us (50%)
  starting transfers between devices  42 us (32%)
  local copies, waits for them, and re-layouts  13.1 us (10%)
  matrix products  4.23 us (3%)
  other arithmetic  3.76 us (3%)
    ppermute x8, waiting for transfers between devices, passed_along(): lax.ppermute(value, axis, [(source, source + steps) for source in range(l...  52.6 us
    ppermute x4, starting transfers between devices, extended(): lax.ppermute(lax.slice_in_dim(block, block.shape[dim] - width, None, axis...  17.8 us
    ppermute x8, starting transfers between devices, passed_along(): lax.ppermute(value, axis, [(source, source + steps) for source in range(l...  17.1 us
    ppermute x4, waiting for transfers between devices, extended(): lax.ppermute(lax.slice_in_dim(block, 0, width, axis=dim), axis, backward)  13.4 us
    ppermute x4, starting transfers between devices, extended(): lax.ppermute(lax.slice_in_dim(block, 0, width, axis=dim), axis, backward)  7.09 us
    unnamed x31, local copies, waits for them, and re-layouts  3.82 us
    dot_general x2, matrix products, conv_pair(): result = jnp.dot(patches, weights, preferred_element_type=jnp.float32)  2.77 us
  transfers between devices with their start and end apart: 16, of which 8 were waited for; matrix products, arithmetic and copies ran while one was open for 1% of the time, Pallas kernels for 0%

commit v1 on v0

v1 whole, which is shorter than its diff:
```python
import jax
import jax.numpy as jnp
from jax import lax
from jax.experimental import pallas as pl
from jax.experimental.pallas import tpu as pltpu
from jax.sharding import PartitionSpec as P

DISP = 512
EDGE = 16
MESH = pl.DeviceIdType.MESH
SIDES = [(-1, 0), (1, 0), (0, -1), (0, 1), (-1, -1), (-1, 1), (1, -1), (1, 1)]
NT = (((1,), (1,)), ((), ()))
TN = (((0,), (0,)), ((), ()))


def guarded(cond, action):
    if cond is True:
        action()
    else:
        pl.when(cond)(action)


def both(first, second):
    if first is True:
        return second
    if second is True:
        return first
    return jnp.logical_and(first, second)


def kernel(
    bands, cols, left_ref, right_ref, kernel_ref, valid_ref, truth_ref, gl_ref, gr_ref,
    image, weights, seg, lfeat, grad, terms, to_partner, to_far, to_near,
    from_partner, from_far, from_near,
    local_sem, halo_send, halo_recv, fwd_send, fwd_recv, rev_send, rev_recv,
):
    band = lax.axis_index("band")
    col = lax.axis_index("col")
    height, columns, channels = left_ref.shape
    reach = DISP // columns
    wide = columns + 2 * EDGE
    factor = channels ** (-0.5)
    even = lax.rem(col, 2) == 0
    odd = jnp.logical_not(even)
    partner = jnp.where(even, col + 1, col - 1)
    images = (left_ref, right_ref)
    pending = []

    def inside(step_b, step_c):
        cond = True
        if step_b < 0:
            cond = both(cond, band + step_b >= 0)
        if step_b > 0:
            cond = both(cond, band + step_b < bands)
        if step_c < 0:
            cond = both(cond, col + step_c >= 0)
        if step_c > 0:
            cond = both(cond, col + step_c < cols)
        return cond

    def send(cond, src, dst, sem_out, sem_in, to_band, to_col):
        def describe():
            return pltpu.make_async_remote_copy(
                src_ref=src, dst_ref=dst, send_sem=sem_out, recv_sem=sem_in,
                device_id={"band": to_band, "col": to_col}, device_id_type=MESH,
            )

        guarded(cond, lambda: describe().start())
        pending.append((cond, describe))

    def arrive(cond, dst, sem_out, sem_in):
        def wait():
            pltpu.make_async_remote_copy(
                src_ref=dst, dst_ref=dst, send_sem=sem_out, recv_sem=sem_in,
                device_id={"band": band, "col": partner}, device_id_type=MESH,
            ).wait_recv()

        guarded(cond, wait)

    def send_span(step, size, edge):
        return (0, edge) if step < 0 else ((size - edge, edge) if step > 0 else (0, size))

    def land_span(step, size, edge):
        return (size + edge, edge) if step < 0 else ((0, edge) if step > 0 else (edge, size))

    def halo_out(source, pad, which, picked=SIDES):
        for side in picked:
            number = SIDES.index(side)
            row, rows = send_span(side[0], height, 1)
            first, count = send_span(side[1], columns, EDGE)
            to_row, _ = land_span(side[0], height, 1)
            to_first, _ = land_span(side[1], columns, EDGE)
            send(
                inside(*side),
                source(row, rows, first, count),
                pad.at[which % 2, pl.ds(to_row, rows), pl.ds(to_first, count)],
                halo_send.at[which, number], halo_recv.at[which, number],
                band + side[0], col + side[1],
            )

    def halo_in(pad, which):
        for number, side in enumerate(SIDES):
            to_row, rows = land_span(side[0], height, 1)
            to_first, count = land_span(side[1], columns, EDGE)
            arrive(
                inside(-side[0], -side[1]),
                pad.at[which % 2, pl.ds(to_row, rows), pl.ds(to_first, count)],
                halo_send.at[which, number], halo_recv.at[which, number],
            )

    def convolve(pad, which, backward):
        rows = [
            pad[which, pl.ds(a, height)].reshape(height * wide, channels) for a in range(3)
        ]
        total = None
        for b in range(3):
            acc = None
            for a in range(3):
                block = weights[pl.ds((3 * a + b) * channels, channels), :]
                if backward:
                    part = lax.dot_general(
                        rows[2 - a], block, NT, preferred_element_type=jnp.float32
                    )
                else:
                    part = jnp.dot(rows[a], block, preferred_element_type=jnp.float32)
                acc = part if acc is None else acc + part
            shift = (b - 1) if backward else (1 - b)
            if shift != 0:
                acc = pltpu.roll(acc, shift % (height * wide), 0)
            total = acc if total is None else total + acc
        total = total.reshape(height, wide, channels)[:, EDGE : EDGE + columns]
        return total.astype(jnp.bfloat16)

    core = (pl.ds(1, height), pl.ds(EDGE, columns))
    locals_in = [
        pltpu.make_async_copy(right_ref, image.at[(1,) + core], local_sem.at[0]),
        pltpu.make_async_copy(left_ref, image.at[(0,) + core], local_sem.at[1]),
        pltpu.make_async_copy(kernel_ref, weights, local_sem.at[2]),
    ]
    for copy in locals_in:
        copy.start()

    for pad in (image, grad):
        for which in range(2):
            for row in (0, height + 1):
                pad[which, row] = jnp.zeros((wide, channels), jnp.bfloat16)
            for first in (0, EDGE + columns):
                pad[which, 1 : height + 1, first : first + EDGE] = jnp.zeros(
                    (height, EDGE, channels), jnp.bfloat16
                )
    for k in range(1, reach + 1):
        @pl.when(col < k)
        def _(k=k):
            seg[:, k] = jnp.zeros((height, columns, channels), jnp.bfloat16)

    barrier = pltpu.get_barrier_semaphore()
    met = jnp.int32(0)
    for side in SIDES + [(0, -2), (0, 2)]:
        cond = inside(*side)

        def greet(side=side):
            pl.semaphore_signal(
                barrier, inc=1,
                device_id={"band": band + side[0], "col": col + side[1]}, device_id_type=MESH,
            )

        guarded(cond, greet)
        met = met + cond.astype(jnp.int32)
    pl.semaphore_wait(barrier, met)

    for which in (1, 0):
        halo_out(
            lambda row, rows, first, count: images[which].at[pl.ds(row, rows), pl.ds(first, count)],
            image, which,
        )
    locals_in[0].wait()
    locals_in[2].wait()
    halo_in(image, 1)
    seg[:, 0] = convolve(image, 1, False)

    two_down, four_down = col >= 2, col >= 4
    two_up = col + 2 < cols
    for r in range(height):
        send(two_up, seg.at[r, 0], seg.at[r, 2], fwd_send.at[0, r], fwd_recv.at[2, r], band, col + 2)
        send(even, seg.at[r, 0], seg.at[r, 1], fwd_send.at[1, r], fwd_recv.at[1, r], band, partner)

    locals_in[1].wait()
    halo_in(image, 0)
    lfeat[...] = convolve(image, 0, False)

    down = lax.broadcasted_iota(jnp.int32, (reach + 1, columns, columns), 1)
    across = lax.broadcasted_iota(jnp.int32, (reach + 1, columns, columns), 2)
    order = lax.broadcasted_iota(jnp.int32, (reach + 1, columns, columns), 0)
    offset = order * columns + across - down
    tall = (reach + 1) * columns

    def pass_near(r):
        arrive(two_down, seg.at[r, 2], fwd_send.at[0, r], fwd_recv.at[2, r])
        send(both(two_down, two_up), seg.at[r, 2], seg.at[r, 4],
             fwd_send.at[2, r], fwd_recv.at[4, r], band, col + 2)
        send(both(two_down, even), seg.at[r, 2], seg.at[r, 3],
             fwd_send.at[3, r], fwd_recv.at[3, r], band, partner)
        send(both(two_down, odd), seg.at[r, 2], seg.at[r, 1],
             fwd_send.at[3, r], fwd_recv.at[1, r], band, partner)

    def pass_far(r):
        arrive(four_down, seg.at[r, 4], fwd_send.at[2, r], fwd_recv.at[4, r])
        send(both(four_down, odd), seg.at[r, 4], seg.at[r, 3],
             fwd_send.at[1, r], fwd_recv.at[3, r], band, partner)

    def correlate(r):
        arrive(jnp.logical_or(odd, two_down), seg.at[r, 1], fwd_send.at[1, r], fwd_recv.at[1, r])
        arrive(jnp.logical_or(both(odd, two_down), four_down), seg.at[r, 3],
               fwd_send.at[3, r], fwd_recv.at[3, r])
        block = seg[r].reshape(tall, channels)
        left = lfeat[r]
        scores = lax.dot_general(block, left, NT, preferred_element_type=jnp.float32) * factor
        scores = scores.reshape(reach + 1, columns, columns)
        distance = (offset - truth_ref[r : r + 1, :].reshape(1, 1, columns)).astype(jnp.float32)
        target = jnp.exp(distance * distance * (-1.0 / 8.0))
        scale = valid_ref[r : r + 1, :].astype(jnp.float32).reshape(1, 1, columns) * (channels / DISP)
        slope = scale * (scores - target)
        slope = jnp.where(jnp.logical_and(offset >= 0, offset < DISP), slope, 0.0)
        slope = slope.astype(jnp.bfloat16).reshape(tall, columns)
        term = jnp.dot(slope, left, preferred_element_type=jnp.float32) * factor
        terms[r] = term.reshape(reach + 1, columns, channels)
        to_partner[r, 0] = terms[r, 1].astype(jnp.bfloat16)
        to_partner[r, 1] = terms[r, 3].astype(jnp.bfloat16)
        send(jnp.logical_or(odd, two_down), to_partner.at[r, 0], from_partner.at[r, 0],
             rev_send.at[0, r], rev_recv.at[0, r], band, partner)
        send(jnp.logical_or(both(odd, two_down), four_down), to_partner.at[r, 1],
             from_partner.at[r, 1], rev_send.at[1, r], rev_recv.at[1, r], band, partner)
        dleft = lax.dot_general(slope, block, TN, preferred_element_type=jnp.float32) * factor
        grad[0, r + 1, pl.ds(EDGE, columns)] = dleft.astype(jnp.bfloat16)

    def add_partner(r, place, k):
        terms[r, k] = terms[r, k] + from_partner[r, place].astype(jnp.float32)

    def return_far(r):
        arrive(jnp.logical_or(even, two_down), from_partner.at[r, 0],
               rev_send.at[0, r], rev_recv.at[0, r])
        arrive(jnp.logical_or(both(even, two_down), four_down), from_partner.at[r, 1],
               rev_send.at[1, r], rev_recv.at[1, r])
        pl.when(both(odd, four_down))(lambda: add_partner(r, 1, 4))
        to_far[r] = terms[r, 4].astype(jnp.bfloat16)
        send(four_down, to_far.at[r], from_far.at[r],
             rev_send.at[2, r], rev_recv.at[2, r], band, col - 2)
        pl.when(both(odd, two_down))(lambda: add_partner(r, 0, 2))
        pl.when(both(even, two_down))(lambda: add_partner(r, 1, 2))
        pl.when(even)(lambda: add_partner(r, 0, 0))

    def return_near(r):
        @pl.when(both(two_down, two_up))
        def _():
            arrive(True, from_far.at[r], rev_send.at[2, r], rev_recv.at[2, r])
            terms[r, 2] = terms[r, 2] + from_far[r].astype(jnp.float32)

        to_near[r] = terms[r, 2].astype(jnp.bfloat16)
        send(two_down, to_near.at[r], from_near.at[r],
             rev_send.at[3, r], rev_recv.at[3, r], band, col - 2)

    def settle(r):
        @pl.when(two_up)
        def _():
            arrive(True, from_near.at[r], rev_send.at[3, r], rev_recv.at[3, r])
            terms[r, 0] = terms[r, 0] + from_near[r].astype(jnp.float32)

        grad[1, r + 1, pl.ds(EDGE, columns)] = terms[r, 0].astype(jnp.bfloat16)

    stages = ((pass_near, 0), (pass_far, 1), (correlate, 1), (return_far, 2), (return_near, 3))
    for step in range(height + 3):
        for stage, lag in stages:
            if 0 <= step - lag < height:
                stage(step - lag)
        if step == height:
            halo_out(
                lambda row, rows, first, count: grad.at[0, pl.ds(1 + row, rows), pl.ds(EDGE + first, count)],
                grad, 2,
            )
    halo_in(grad, 2)
    gl_ref[...] = convolve(grad, 0, True)
    for r in range(height):
        settle(r)
    halo_out(
        lambda row, rows, first, count: grad.at[1, pl.ds(1 + row, rows), pl.ds(EDGE + first, count)],
        grad, 3,
    )
    halo_in(grad, 3)
    gr_ref[...] = convolve(grad, 1, True)
    for cond, describe in pending:
        guarded(cond, lambda: describe().wait_send())


def solution(mesh):
    bands, cols = mesh.shape["band"], mesh.shape["col"]

    def shards(left_image, right_image, weights, valid_mask, disparity):
        height, columns, channels = left_image.shape
        reach = DISP // columns
        wide = columns + 2 * EDGE
        bf16 = jnp.bfloat16
        any_spec = pl.BlockSpec(memory_space=pl.ANY)
        vmem_spec = pl.BlockSpec(memory_space=pltpu.VMEM)
        dma = pltpu.SemaphoreType.DMA
        pad = pltpu.VMEM((2, height + 2, wide, channels), bf16)
        rows = pltpu.VMEM((height, columns, channels), bf16)
        pairs = pltpu.VMEM((height, 2, columns, channels), bf16)

        def body(*refs):
            kernel(bands, cols, *refs)

        return pl.pallas_call(
            body,
            out_shape=(
                jax.ShapeDtypeStruct(left_image.shape, bf16),
                jax.ShapeDtypeStruct(right_image.shape, bf16),
            ),
            in_specs=[any_spec, any_spec, any_spec, vmem_spec, vmem_spec],
            out_specs=(vmem_spec, vmem_spec),
            scratch_shapes=[
                pad,
                pltpu.VMEM(weights.shape, bf16),
                pltpu.VMEM((height, reach + 1, columns, channels), bf16),
                rows,
                pad,
                pltpu.VMEM((height, reach + 1, columns, channels), jnp.float32),
                pairs, rows, rows,
                pairs, rows, rows,
                dma((3,)),
                dma((4, 8)), dma((4, 8)),
                dma((4, height)), dma((reach + 1, height)),
                dma((4, height)), dma((4, height)),
            ],
            compiler_params=pltpu.CompilerParams(
                collective_id=0, has_side_effects=True, vmem_limit_bytes=48 * 2**20
            ),
            cost_estimate=pl.CostEstimate(
                flops=5_000_000_000, bytes_accessed=4_000_000, transcendentals=400_000
            ),
        )(left_image, right_image, weights, valid_mask, disparity)

    return jax.shard_map(
        shards,
        mesh=mesh,
        in_specs=(
            P("band", "col", None),
            P("band", "col", None),
            P(),
            P("band", "col"),
            P("band", "col"),
        ),
        out_specs=(P("band", "col", None), P("band", "col", None)),
        check_vma=False,
    )
```

time: 131 us -> 64.1 us (0.49)
  waiting for transfers between devices: 66.1 us -> 0 us
  Pallas kernels: 0 us -> 57.2 us
  starting transfers between devices: 42 us -> 0 us
  local copies, waits for them, and re-layouts: 13.1 us -> 5.93 us
  matrix products: 4.23 us -> 0 us
  other arithmetic: 3.76 us -> 0 us
    ppermute x16 -> x0, waiting for transfers between devices: 66.1 us -> none  [the longest x8 52.6 us: passed_along(): lax.ppermute(value, axis, [(source, source + steps) for source in range(l...]
    pallas_call x0 -> x1, Pallas kernels: none -> 57.2 us  [shards(): pl.pallas_call(body, out_shape=(jax.ShapeDtypeStruct(left_image.shape, bf...]
    ppermute x16 -> x0, starting transfers between devices: 42 us -> none  [the longest x4 17.8 us: extended(): lax.ppermute(lax.slice_in_dim(block, block.shape[dim] - width, None, axis...]
    dot_general x5 -> x0, matrix products: 4.23 us -> none  [the longest x2 2.77 us: conv_pair(): result = jnp.dot(patches, weights, preferred_element_type=jnp.float32)]
    reshape x2 -> x0, local copies, waits for them, and re-layouts: 3.2 us -> none  [the longest x1 1.62 us: band_to_diagonals(): return flattened.reshape(height, columns, extent + 1)[:, :, 1:reach + 1]]
    rev x2 -> x0, local copies, waits for them, and re-layouts: 3.14 us -> none  [the longest x1 1.65 us: shards(): banded = diagonals_to_band(gradient[:, :, ::-1], DISP)]
    unnamed x31 -> x12, local copies, waits for them, and re-layouts: 3.82 us -> 5.93 us
    concatenate x5 -> x0, other arithmetic: 1.87 us -> none  [the longest x4 1.49 us: extended(): block = jnp.concatenate([low, block, high], axis=dim)]
  transfers between devices with their start and end apart: 16 -> 0, of which waited for: 8 -> 0; matrix products, arithmetic and copies ran while one was open for 1% -> 0% of each run, Pallas kernels for 0% -> 0%
where the time goes in v1:
time: 64.1 us; the launch traced here: 63.8 us
  Pallas kernels  57.2 us (89%)
  local copies, waits for them, and re-layouts  5.93 us (9%)
  between operations  0.65 us (1%)
    pallas_call x1, Pallas kernels, shards(): pl.pallas_call(body, out_shape=(jax.ShapeDtypeStruct(left_image.shape, bf...  57.2 us
    unnamed x12, local copies, waits for them, and re-layouts  5.93 us

profile of v1, /device:TPU:1, one launch (start us, length us, event | category | flops | bytes accessed | tf_op | source)
XLA Modules:
  0.0 63.8 jit_solution(3709354253894157245)
XLA Ops:
  0.6 0.0 copy-start
  0.6 1.3 %copy-done = bf16[2304,256]{1,0:T(8,128)(2,1)S(1)} copy-done((bf16[2304,256]{1,0:T(8,128)(2,1)S(1)}, bf16[2304,256]{1,0:T(8,128)(2,1)}, u32[]{:S(2)}) %copy-start) | copy-done | bytes 1179672
  1.9 0.0 copy-start.1
  1.9 0.9 %copy-done.1 = bf16[4,128,256]{2,1,0:T(8,128)(2,1)S(1)} copy-done((bf16[4,128,256]{2,1,0:T(8,128)(2,1)S(1)}, bf16[4,128,256]{2,1,0:T(8,128)(2,1)}, u32[]{:S(2)}) %copy-start.1) | copy-done | bytes 262168
  2.9 0.0 copy-start.2
  2.9 0.9 %copy-done.2 = bf16[4,128,256]{2,1,0:T(8,128)(2,1)S(1)} copy-done((bf16[4,128,256]{2,1,0:T(8,128)(2,1)S(1)}, bf16[4,128,256]{2,1,0:T(8,128)(2,1)}, u32[]{:S(2)}) %copy-start.2) | copy-done | bytes 262168
  3.8 0.0 copy-start.3
  3.8 0.7 %copy-done.3 = s32[4,128]{1,0:T(4,128)S(1)} copy-done((s32[4,128]{1,0:T(4,128)S(1)}, s32[4,128]{1,0:T(4,128)}, u32[]{:S(2)}) %copy-start.3) | copy-done | bytes 2072
  4.5 0.0 copy-start.4
  4.5 0.7 %copy-done.4 = s32[4,128]{1,0:T(4,128)S(1)} copy-done((s32[4,128]{1,0:T(4,128)S(1)}, s32[4,128]{1,0:T(4,128)}, u32[]{:S(2)}) %copy-start.4) | copy-done | bytes 2072
  5.2 57.2 %shard_map.68 = (bf16[4,128,256]{2,1,0:T(8,128)(2,1)S(1)}, bf16[4,128,256]{2,1,0:T(8,128)(2,1)S(1)}) custom-call(bf16[4,128,256]{2,1,0:T(8,128)(2,1)S(1)} %copy-done.1, bf16[4,128,256]{2,1,0:T(8,128)(2,1)S(1)} %copy-done.2, bf16[2304,256]{1,0:T(8,128)(2,1)S(1)} %copy-done, s32[4,128]{1,0:T(4,128)S(1)} %copy-done.3, s32[4,128]{1,0:T(4,128)S(1)} %copy-done.4), custom_call_target="tpu_custom_call" | custom-call | flops 5000000000 | bytes 4000000 | tf_op jit(solution)/shard_map/pallas_call | solution.py:312
  62.4 0.7 %copy.9 = bf16[4,128,256]{2,1,0:T(8,128)(2,1)} copy(bf16[4,128,256]{2,1,0:T(8,128)(2,1)S(1)} %get-tuple-element.4) | data formatting | bytes 524288
  63.1 0.7 %copy.10 = bf16[4,128,256]{2,1,0:T(8,128)(2,1)} copy(bf16[4,128,256]{2,1,0:T(8,128)(2,1)S(1)} %get-tuple-element.5) | data formatting | bytes 524288
Async XLA Ops:
  0.6 1.3 %copy-start = (bf16[2304,256]{1,0:T(8,128)(2,1)S(1)}, bf16[2304,256]{1,0:T(8,128)(2,1)}, u32[]{:S(2)}) copy-start(bf16[2304,256]{1,0:T(8,128)(2,1)} %refs_2_.1) | copy-start | bytes 3538948
  1.9 0.9 %copy-start.1 = (bf16[4,128,256]{2,1,0:T(8,128)(2,1)S(1)}, bf16[4,128,256]{2,1,0:T(8,128)(2,1)}, u32[]{:S(2)}) copy-start(bf16[4,128,256]{2,1,0:T(8,128)(2,1)} %refs_0_.1) | copy-start | bytes 786436
  2.9 0.9 %copy-start.2 = (bf16[4,128,256]{2,1,0:T(8,128)(2,1)S(1)}, bf16[4,128,256]{2,1,0:T(8,128)(2,1)}, u32[]{:S(2)}) copy-start(bf16[4,128,256]{2,1,0:T(8,128)(2,1)} %refs_1_.1) | copy-start | bytes 786436
  3.8 0.7 %copy-start.3 = (s32[4,128]{1,0:T(4,128)S(1)}, s32[4,128]{1,0:T(4,128)}, u32[]{:S(2)}) copy-start(s32[4,128]{1,0:T(4,128)} %refs_3_.1) | copy-start | bytes 6148
  4.5 0.7 %copy-start.4 = (s32[4,128]{1,0:T(4,128)S(1)}, s32[4,128]{1,0:T(4,128)}, u32[]{:S(2)}) copy-start(s32[4,128]{1,0:T(4,128)} %refs_4_.1) | copy-start | bytes 6148

commit v2 on v1

v2 whole, which is shorter than its diff:
```python
import jax
import jax.numpy as jnp
from jax import lax
from jax.experimental import pallas as pl
from jax.experimental.pallas import tpu as pltpu
from jax.sharding import PartitionSpec as P

DISP = 512
EDGE = 16
MESH = pl.DeviceIdType.MESH
SIDES = [(-1, 0), (1, 0), (0, -1), (0, 1), (-1, -1), (-1, 1), (1, -1), (1, 1)]
NT = (((1,), (1,)), ((), ()))
TN = (((0,), (0,)), ((), ()))


def guarded(cond, action):
    if cond is True:
        action()
    else:
        pl.when(cond)(action)


def both(first, second):
    if first is True:
        return second
    if second is True:
        return first
    return jnp.logical_and(first, second)


def kernel(
    bands, cols, left_ref, right_ref, kernel_ref, valid_ref, truth_ref, gl_ref, gr_ref,
    image, weights, truth, valid, seg, lfeat, left_sum, grad, terms, results,
    to_partner, to_far, to_near, from_partner, from_far, from_near,
    local_sem, halo_send, halo_recv, fwd_send, fwd_recv, rev_send, rev_recv,
    left_send, left_recv, side_send, side_recv,
):
    band = lax.axis_index("band")
    col = lax.axis_index("col")
    height, columns, channels = left_ref.shape
    slots = DISP // columns // 2 + 1
    wide = columns + 2 * EDGE
    factor = channels ** (-0.5)
    even = lax.rem(col, 2) == 0
    odd = jnp.logical_not(even)
    partner = jnp.where(even, col + 1, col - 1)
    images = (left_ref, right_ref)
    pending = []

    def inside(step_b, step_c):
        cond = True
        if step_b < 0:
            cond = both(cond, band + step_b >= 0)
        if step_b > 0:
            cond = both(cond, band + step_b < bands)
        if step_c < 0:
            cond = both(cond, col + step_c >= 0)
        if step_c > 0:
            cond = both(cond, col + step_c < cols)
        return cond

    def send(cond, src, dst, sem_out, sem_in, to_band, to_col):
        def describe():
            return pltpu.make_async_remote_copy(
                src_ref=src, dst_ref=dst, send_sem=sem_out, recv_sem=sem_in,
                device_id={"band": to_band, "col": to_col}, device_id_type=MESH,
            )

        guarded(cond, lambda: describe().start())
        pending.append((cond, describe))

    def arrive(cond, dst, sem_out, sem_in):
        def wait():
            pltpu.make_async_remote_copy(
                src_ref=dst, dst_ref=dst, send_sem=sem_out, recv_sem=sem_in,
                device_id={"band": band, "col": partner}, device_id_type=MESH,
            ).wait_recv()

        guarded(cond, wait)

    def send_span(step, size, edge):
        return (0, edge) if step < 0 else ((size - edge, edge) if step > 0 else (0, size))

    def land_span(step, size, edge):
        return (size + edge, edge) if step < 0 else ((0, edge) if step > 0 else (edge, size))

    def halo_out(source, pad, which, picked=SIDES):
        for side in picked:
            number = SIDES.index(side)
            row, rows = send_span(side[0], height, 1)
            first, count = send_span(side[1], columns, EDGE)
            to_row, _ = land_span(side[0], height, 1)
            to_first, _ = land_span(side[1], columns, EDGE)
            send(
                inside(*side),
                source(row, rows, first, count),
                pad.at[which % 2, pl.ds(to_row, rows), pl.ds(to_first, count)],
                halo_send.at[which, number], halo_recv.at[which, number],
                band + side[0], col + side[1],
            )

    def halo_in(pad, which):
        for number, side in enumerate(SIDES):
            to_row, rows = land_span(side[0], height, 1)
            to_first, count = land_span(side[1], columns, EDGE)
            arrive(
                inside(-side[0], -side[1]),
                pad.at[which % 2, pl.ds(to_row, rows), pl.ds(to_first, count)],
                halo_send.at[which, number], halo_recv.at[which, number],
            )

    def convolve(pad, which, backward):
        rows = [
            pad[which, pl.ds(a, height)].reshape(height * wide, channels) for a in range(3)
        ]
        total = None
        for b in range(3):
            acc = None
            for a in range(3):
                block = weights[pl.ds((3 * a + b) * channels, channels), :]
                if backward:
                    part = lax.dot_general(
                        rows[2 - a], block, NT, preferred_element_type=jnp.float32
                    )
                else:
                    part = jnp.dot(rows[a], block, preferred_element_type=jnp.float32)
                acc = part if acc is None else acc + part
            shift = (b - 1) if backward else (1 - b)
            if shift != 0:
                acc = pltpu.roll(acc, shift % (height * wide), 0)
            total = acc if total is None else total + acc
        total = total.reshape(height, wide, channels)[:, EDGE : EDGE + columns]
        return total.astype(jnp.bfloat16)

    core = (pl.ds(1, height), pl.ds(EDGE, columns))
    locals_in = [
        pltpu.make_async_copy(right_ref, image.at[(1,) + core], local_sem.at[0]),
        pltpu.make_async_copy(left_ref, image.at[(0,) + core], local_sem.at[1]),
        pltpu.make_async_copy(kernel_ref, weights, local_sem.at[2]),
        pltpu.make_async_copy(truth_ref, truth.at[0], local_sem.at[3]),
        pltpu.make_async_copy(valid_ref, valid.at[0], local_sem.at[4]),
    ]
    for copy in locals_in:
        copy.start()

    for pad in (image, grad):
        for which in range(2):
            for row in (0, height + 1):
                pad[which, row] = jnp.zeros((wide, channels), jnp.bfloat16)
            for first in (0, EDGE + columns):
                pad[which, 1 : height + 1, first : first + EDGE] = jnp.zeros(
                    (height, EDGE, channels), jnp.bfloat16
                )
    for k in range(1, slots):
        @pl.when(col < 2 * k)
        def _(k=k):
            seg[:, k] = jnp.zeros((height, columns, channels), jnp.bfloat16)

    barrier = pltpu.get_barrier_semaphore()
    met = jnp.int32(0)
    for side in SIDES + [(0, -2), (0, 2)]:
        cond = inside(*side)

        def greet(side=side):
            pl.semaphore_signal(
                barrier, inc=1,
                device_id={"band": band + side[0], "col": col + side[1]}, device_id_type=MESH,
            )

        guarded(cond, greet)
        met = met + cond.astype(jnp.int32)
    pl.semaphore_wait(barrier, met)

    for which in (1, 0):
        halo_out(
            lambda row, rows, first, count: images[which].at[pl.ds(row, rows), pl.ds(first, count)],
            image, which,
        )
    send(True, truth_ref, truth.at[1], side_send.at[0], side_recv.at[0], band, partner)
    send(True, valid_ref, valid.at[1], side_send.at[1], side_recv.at[1], band, partner)
    locals_in[0].wait()
    locals_in[2].wait()
    halo_in(image, 1)
    seg[:, 0] = convolve(image, 1, False)

    two_down, four_down = col >= 2, col >= 4
    two_up = col + 2 < cols

    def own_up(r):
        send(two_up, seg.at[r, 0], seg.at[r, 1], fwd_send.at[0, r], fwd_recv.at[0, r], band, col + 2)

    own_up(0)
    own_up(1)
    locals_in[1].wait()
    halo_in(image, 0)
    lfeat[0] = convolve(image, 0, False)
    for r in range(height):
        send(True, lfeat.at[0, r], lfeat.at[1, r], left_send.at[0, r], left_recv.at[0, r], band, partner)
    for copy in locals_in[3:]:
        copy.wait()
    arrive(True, truth.at[1], side_send.at[0], side_recv.at[0])
    arrive(True, valid.at[1], side_send.at[1], side_recv.at[1])

    odd_slot = odd.astype(jnp.int32)

    def pass_near(r):
        arrive(two_down, seg.at[r, 1], fwd_send.at[0, r], fwd_recv.at[0, r])
        send(both(two_down, two_up), seg.at[r, 1], seg.at[r, 2],
             fwd_send.at[1, r], fwd_recv.at[1, r], band, col + 2)
        if r + 2 < height:
            own_up(r + 2)

    def slopes(r, who, block, first, count):
        shape = (count, columns, columns)
        offset = (
            (2 * lax.broadcasted_iota(jnp.int32, shape, 0) + first) * columns
            + lax.broadcasted_iota(jnp.int32, shape, 2)
            - lax.broadcasted_iota(jnp.int32, shape, 1)
        )
        left = lfeat[who, r]
        scores = lax.dot_general(block, left, NT, preferred_element_type=jnp.float32) * factor
        scores = scores.reshape(shape)
        distance = (offset - truth[who, r : r + 1, :].reshape(1, 1, columns)).astype(jnp.float32)
        target = jnp.exp(distance * distance * (-1.0 / 8.0))
        scale = valid[who, r : r + 1, :].astype(jnp.float32).reshape(1, 1, columns)
        slope = scale * (scores - target) * (channels / DISP)
        slope = jnp.where(jnp.logical_and(offset >= 0, offset < DISP), slope, 0.0)
        slope = slope.astype(jnp.bfloat16).reshape(count * columns, columns)
        term = jnp.dot(slope, left, preferred_element_type=jnp.float32) * factor
        dleft = lax.dot_general(slope, block, TN, preferred_element_type=jnp.float32) * factor
        return term.reshape(count, columns, channels), dleft

    def correlate(r):
        arrive(four_down, seg.at[r, 2], fwd_send.at[1, r], fwd_recv.at[1, r])
        arrive(True, lfeat.at[1, r], left_send.at[0, r], left_recv.at[0, r])
        block = seg[r, pl.ds(odd_slot, slots - 1)].reshape((slots - 1) * columns, channels)
        other, other_left = slopes(r, 1, block, 1, slots - 1)
        to_partner[r] = other_left.astype(jnp.bfloat16)
        send(True, to_partner.at[r], from_partner.at[r],
             left_send.at[1, r], left_recv.at[1, r], band, partner)
        own, own_left = slopes(r, 0, seg[r].reshape(slots * columns, channels), 0, slots)
        terms[r] = own
        terms[r, pl.ds(odd_slot, slots - 1)] = terms[r, pl.ds(odd_slot, slots - 1)] + other
        to_far[r] = terms[r, 2].astype(jnp.bfloat16)
        send(four_down, to_far.at[r], from_far.at[r],
             rev_send.at[0, r], rev_recv.at[0, r], band, col - 2)
        left_sum[r] = own_left

    def return_near(r):
        @pl.when(both(two_down, two_up))
        def _():
            arrive(True, from_far.at[r], rev_send.at[0, r], rev_recv.at[0, r])
            terms[r, 1] = terms[r, 1] + from_far[r].astype(jnp.float32)

        to_near[r] = terms[r, 1].astype(jnp.bfloat16)
        send(two_down, to_near.at[r], from_near.at[r],
             rev_send.at[1, r], rev_recv.at[1, r], band, col - 2)

    def settle_left(r):
        arrive(True, from_partner.at[r], left_send.at[1, r], left_recv.at[1, r])
        total = left_sum[r] + from_partner[r].astype(jnp.float32)
        grad[0, r + 1, pl.ds(EDGE, columns)] = total.astype(jnp.bfloat16)

    def settle(r):
        @pl.when(two_up)
        def _():
            arrive(True, from_near.at[r], rev_send.at[1, r], rev_recv.at[1, r])
            terms[r, 0] = terms[r, 0] + from_near[r].astype(jnp.float32)

        grad[1, r + 1, pl.ds(EDGE, columns)] = terms[r, 0].astype(jnp.bfloat16)

    def grads_out(which):
        halo_out(
            lambda row, rows, first, count: grad.at[which, pl.ds(1 + row, rows), pl.ds(EDGE + first, count)],
            grad, 2 + which,
        )

    stages = ((pass_near, 0), (correlate, 1), (return_near, 2))
    for step in range(height + 2):
        for stage, lag in stages:
            if 0 <= step - lag < height:
                stage(step - lag)
    for r in range(height):
        settle_left(r)
    grads_out(0)
    for r in range(height):
        settle(r)
    grads_out(1)
    halo_in(grad, 2)
    results[0] = convolve(grad, 0, True)
    out_left = pltpu.make_async_copy(results.at[0], gl_ref, local_sem.at[5])
    out_left.start()
    halo_in(grad, 3)
    results[1] = convolve(grad, 1, True)
    out_right = pltpu.make_async_copy(results.at[1], gr_ref, local_sem.at[6])
    out_right.start()
    for cond, describe in pending:
        guarded(cond, lambda: describe().wait_send())
    out_left.wait()
    out_right.wait()


def solution(mesh):
    bands, cols = mesh.shape["band"], mesh.shape["col"]

    def shards(left_image, right_image, weights, valid_mask, disparity):
        height, columns, channels = left_image.shape
        slots = DISP // columns // 2 + 1
        wide = columns + 2 * EDGE
        bf16 = jnp.bfloat16
        any_spec = pl.BlockSpec(memory_space=pl.ANY)
        dma = pltpu.SemaphoreType.DMA
        pad = pltpu.VMEM((2, height + 2, wide, channels), bf16)
        rows = pltpu.VMEM((height, columns, channels), bf16)
        both_rows = pltpu.VMEM((2, height, columns, channels), bf16)
        pixels = pltpu.VMEM((2, height, columns), jnp.int32)

        def body(*refs):
            kernel(bands, cols, *refs)

        return pl.pallas_call(
            body,
            out_shape=(
                jax.ShapeDtypeStruct(left_image.shape, bf16),
                jax.ShapeDtypeStruct(right_image.shape, bf16),
            ),
            in_specs=[any_spec] * 5,
            out_specs=(any_spec, any_spec),
            scratch_shapes=[
                pad,
                pltpu.VMEM(weights.shape, bf16),
                pixels, pixels,
                pltpu.VMEM((height, slots, columns, channels), bf16),
                both_rows,
                pltpu.VMEM((height, columns, channels), jnp.float32),
                pad,
                pltpu.VMEM((height, slots, columns, channels), jnp.float32),
                both_rows,
                rows, rows, rows,
                rows, rows, rows,
                dma((7,)),
                dma((4, 8)), dma((4, 8)),
                dma((2, height)), dma((2, height)),
                dma((2, height)), dma((2, height)),
                dma((2, height)), dma((2, height)),
                dma((2,)), dma((2,)),
            ],
            compiler_params=pltpu.CompilerParams(
                collective_id=0, has_side_effects=True, vmem_limit_bytes=60 * 2**20
            ),
            cost_estimate=pl.CostEstimate(
                flops=5_000_000_000, bytes_accessed=4_000_000, transcendentals=400_000
            ),
        )(left_image, right_image, weights, valid_mask, disparity)

    return jax.shard_map(
        shards,
        mesh=mesh,
        in_specs=(
            P("band", "col", None),
            P("band", "col", None),
            P(),
            P("band", "col"),
            P("band", "col"),
        ),
        out_specs=(P("band", "col", None), P("band", "col", None)),
        check_vma=False,
    )
```

time: 64.1 us -> 44.3 us (0.69)
  Pallas kernels: 57.2 us -> 40.1 us
  local copies, waits for them, and re-layouts: 5.93 us -> 3.34 us
    pallas_call x1, Pallas kernels: 57.2 us -> 40.1 us  [shards(): pl.pallas_call(body, out_shape=(jax.ShapeDtypeStruct(left_image.shape, bf...]
    unnamed x12 -> x2, local copies, waits for them, and re-layouts: 5.93 us -> 3.34 us
where the time goes in v2:
time: 44.3 us; the launch traced here: 44.1 us
  Pallas kernels  40.1 us (91%)
  local copies, waits for them, and re-layouts  3.34 us (8%)
  between operations  0.64 us (1%)
    pallas_call x1, Pallas kernels, shards(): pl.pallas_call(body, out_shape=(jax.ShapeDtypeStruct(left_image.shape, bf...  40.1 us
    unnamed x2, local copies, waits for them, and re-layouts  3.34 us

profile of v2, /device:TPU:1, one launch (start us, length us, event | category | flops | bytes accessed | tf_op | source)
XLA Modules:
  0.0 44.1 jit_solution(145416176307064421)
XLA Ops:
  0.6 40.1 %shard_map.68 = (bf16[4,128,256]{2,1,0:T(8,128)(2,1)}, bf16[4,128,256]{2,1,0:T(8,128)(2,1)}) custom-call(bf16[4,128,256]{2,1,0:T(8,128)(2,1)} %refs_0_.1, bf16[4,128,256]{2,1,0:T(8,128)(2,1)} %refs_1_.1, bf16[2304,256]{1,0:T(8,128)(2,1)} %refs_2_.1, s32[4,128]{1,0:T(4,128)} %refs_3_.1, s32[4,128]{1,0:T(4,128)} %refs_4_.1), custom_call_target="tpu_custom_call" | custom-call | flops 5000000000 | bytes 4000000 | tf_op jit(solution)/shard_map/pallas_call | solution.py:321
  40.8 1.7 %copy.9 = bf16[4,128,256]{2,1,0:T(8,128)(2,1)} copy(bf16[4,128,256]{2,1,0:T(8,128)(2,1)} %get-tuple-element.4) | data formatting | bytes 524288
  42.4 1.7 %copy.10 = bf16[4,128,256]{2,1,0:T(8,128)(2,1)} copy(bf16[4,128,256]{2,1,0:T(8,128)(2,1)} %get-tuple-element.5) | data formatting | bytes 524288

commit v3 on v2

--- a/solution.py
+++ b/solution.py
@@ -30,7 +30,7 @@
 
 def kernel(
     bands, cols, left_ref, right_ref, kernel_ref, valid_ref, truth_ref, gl_ref, gr_ref,
-    image, weights, truth, valid, seg, lfeat, left_sum, grad, terms, results,
+    image, weights, flipped, truth, valid, seg, lfeat, left_sum, grad, terms, results,
     to_partner, to_far, to_near, from_partner, from_far, from_near,
     local_sem, halo_send, halo_recv, fwd_send, fwd_recv, rev_send, rev_recv,
     left_send, left_recv, side_send, side_recv,
@@ -110,27 +110,30 @@
             )
 
     def convolve(pad, which, backward):
-        rows = [
-            pad[which, pl.ds(a, height)].reshape(height * wide, channels) for a in range(3)
-        ]
+        spans = ((0, EDGE + columns), (EDGE, columns), (EDGE, columns + EDGE))
         total = None
-        for b in range(3):
-            acc = None
-            for a in range(3):
-                block = weights[pl.ds((3 * a + b) * channels, channels), :]
-                if backward:
-                    part = lax.dot_general(
-                        rows[2 - a], block, NT, preferred_element_type=jnp.float32
-                    )
-                else:
-                    part = jnp.dot(rows[a], block, preferred_element_type=jnp.float32)
-                acc = part if acc is None else acc + part
-            shift = (b - 1) if backward else (1 - b)
-            if shift != 0:
-                acc = pltpu.roll(acc, shift % (height * wide), 0)
-            total = acc if total is None else total + acc
-        total = total.reshape(height, wide, channels)[:, EDGE : EDGE + columns]
-        return total.astype(jnp.bfloat16)
+        for b in (1, 0, 2):
+            side = 2 - b if backward else b
+            first, count = spans[side]
+            lines = jnp.concatenate(
+                [
+                    pad[which, pl.ds(2 - a if backward else a, height), pl.ds(first, count)]
+                    .reshape(height * count, channels)
+                    for a in range(3)
+                ],
+                1,
+            )
+            source = flipped if backward else weights
+            blocks = jnp.concatenate(
+                [source[pl.ds((3 * a + b) * channels, channels), :] for a in range(3)], 0
+            )
+            part = jnp.dot(lines, blocks, preferred_element_type=jnp.float32)
+            if side != 1:
+                part = pltpu.roll(part, (1 - side) % (height * count), 0)
+            part = part.reshape(height, count, channels)
+            part = part[:, EDGE:] if side == 0 else part[:, :columns]
+            total = part if total is None else total + part
+        return total
 
     core = (pl.ds(1, height), pl.ds(EDGE, columns))
     locals_in = [
@@ -180,8 +183,11 @@
     send(True, valid_ref, valid.at[1], side_send.at[1], side_recv.at[1], band, partner)
     locals_in[0].wait()
     locals_in[2].wait()
+    for position in range(9):
+        place = pl.ds(position * channels, channels)
+        flipped[place, :] = weights[place, :].T
     halo_in(image, 1)
-    seg[:, 0] = convolve(image, 1, False)
+    seg[:, 0] = convolve(image, 1, False).astype(jnp.bfloat16)
 
     two_down, four_down = col >= 2, col >= 4
     two_up = col + 2 < cols
@@ -193,7 +199,7 @@
     own_up(1)
     locals_in[1].wait()
     halo_in(image, 0)
-    lfeat[0] = convolve(image, 0, False)
+    lfeat[0] = convolve(image, 0, False).astype(jnp.bfloat16)
     for r in range(height):
         send(True, lfeat.at[0, r], lfeat.at[1, r], left_send.at[0, r], left_recv.at[0, r], band, partner)
     for copy in locals_in[3:]:
@@ -275,14 +281,15 @@
             grad, 2 + which,
         )
 
-    stages = ((pass_near, 0), (correlate, 1), (return_near, 2))
-    for step in range(height + 2):
+    stages = ((pass_near, 0), (correlate, 1), (return_near, 3))
+    for step in range(height + 3):
         for stage, lag in stages:
             if 0 <= step - lag < height:
                 stage(step - lag)
-    for r in range(height):
-        settle_left(r)
-    grads_out(0)
+        if step == height:
+            for r in range(height):
+                settle_left(r)
+            grads_out(0)
     for r in range(height):
         settle(r)
     grads_out(1)
@@ -318,16 +325,17 @@
         def body(*refs):
             kernel(bands, cols, *refs)
 
-        return pl.pallas_call(
+        grad_left, grad_right = pl.pallas_call(
             body,
             out_shape=(
-                jax.ShapeDtypeStruct(left_image.shape, bf16),
-                jax.ShapeDtypeStruct(right_image.shape, bf16),
+                jax.ShapeDtypeStruct(left_image.shape, jnp.float32),
+                jax.ShapeDtypeStruct(right_image.shape, jnp.float32),
             ),
             in_specs=[any_spec] * 5,
             out_specs=(any_spec, any_spec),
             scratch_shapes=[
                 pad,
+                pltpu.VMEM(weights.shape, bf16),
                 pltpu.VMEM(weights.shape, bf16),
                 pixels, pixels,
                 pltpu.VMEM((height, slots, columns, channels), bf16),
@@ -335,7 +343,7 @@
                 pltpu.VMEM((height, columns, channels), jnp.float32),
                 pad,
                 pltpu.VMEM((height, slots, columns, channels), jnp.float32),
-                both_rows,
+                pltpu.VMEM((2, height, columns, channels), jnp.float32),
                 rows, rows, rows,
                 rows, rows, rows,
                 dma((7,)),
@@ -352,6 +360,7 @@
                 flops=5_000_000_000, bytes_accessed=4_000_000, transcendentals=400_000
             ),
         )(left_image, right_image, weights, valid_mask, disparity)
+        return grad_left.astype(bf16), grad_right.astype(bf16)
 
     return jax.shard_map(
         shards,

time: 44.3 us -> 44.3 us (level)
  other arithmetic: 0 us -> 3.54 us
  local copies, waits for them, and re-layouts: 3.34 us -> 0 us
    convert_element_type x0 -> x2, other arithmetic: none -> 3.54 us  [shards(): return (grad_left.astype(bf16), grad_right.astype(bf16))]
    unnamed x2 -> x0, local copies, waits for them, and re-layouts: 3.34 us -> none
where the time goes in v3:
time: 44.3 us; the launch traced here: 44.1 us
  Pallas kernels  39.9 us (90%)
  other arithmetic  3.54 us (8%)
  between operations  0.64 us (1%)
    pallas_call x1, Pallas kernels, shards(): pl.pallas_call(body, out_shape=(jax.ShapeDtypeStruct(left_image.shape, jn...  39.9 us
    convert_element_type x2, other arithmetic, shards(): return (grad_left.astype(bf16), grad_right.astype(bf16))  3.54 us

profile of v3, /device:TPU:1, one launch (start us, length us, event | category | flops | bytes accessed | tf_op | source)
XLA Modules:
  0.0 44.1 jit_solution(11430842018118453806)
XLA Ops:
  0.6 39.9 %shard_map.68 = (f32[4,128,256]{2,1,0:T(8,128)}, f32[4,128,256]{2,1,0:T(8,128)}) custom-call(bf16[4,128,256]{2,1,0:T(8,128)(2,1)} %refs_0_.1, bf16[4,128,256]{2,1,0:T(8,128)(2,1)} %refs_1_.1, bf16[2304,256]{1,0:T(8,128)(2,1)} %refs_2_.1, s32[4,128]{1,0:T(4,128)} %refs_3_.1, s32[4,128]{1,0:T(4,128)} %refs_4_.1), custom_call_target="tpu_custom_call" | custom-call | flops 5000000000 | bytes 4000000 | tf_op jit(solution)/shard_map/pallas_call | solution.py:328
  40.6 1.8 %convert_element_type.6 = bf16[4,128,256]{2,1,0:T(8,128)(2,1)} convert(f32[4,128,256]{2,1,0:T(8,128)} %get-tuple-element.4) | non-fusion elementwise | flops 131072 | bytes 786432 | tf_op jit(solution)/shard_map/convert_element_type | solution.py:363
  42.4 1.8 %convert_element_type.7 = bf16[4,128,256]{2,1,0:T(8,128)(2,1)} convert(f32[4,128,256]{2,1,0:T(8,128)} %get-tuple-element.5) | non-fusion elementwise | flops 131072 | bytes 786432 | tf_op jit(solution)/shard_map/convert_element_type | solution.py:363

commit v4 on v3

--- a/solution.py
+++ b/solution.py
@@ -294,17 +294,30 @@
         settle(r)
     grads_out(1)
     halo_in(grad, 2)
-    results[0] = convolve(grad, 0, True)
+    results[0] = convolve(grad, 0, True).astype(jnp.bfloat16)
     out_left = pltpu.make_async_copy(results.at[0], gl_ref, local_sem.at[5])
     out_left.start()
     halo_in(grad, 3)
-    results[1] = convolve(grad, 1, True)
+    results[1] = convolve(grad, 1, True).astype(jnp.bfloat16)
     out_right = pltpu.make_async_copy(results.at[1], gr_ref, local_sem.at[6])
     out_right.start()
     for cond, describe in pending:
         guarded(cond, lambda: describe().wait_send())
     out_left.wait()
     out_right.wait()
+
+
+def hand_out(left_ref, right_ref, gl_ref, gr_ref, sems):
+    height = left_ref.shape[0]
+    copies = [
+        pltpu.make_async_copy(source.at[r], target.at[r], sems.at[which, r])
+        for r in range(height)
+        for which, (source, target) in enumerate(((left_ref, gl_ref), (right_ref, gr_ref)))
+    ]
+    for copy in copies:
+        copy.start()
+    for copy in copies:
+        copy.wait()
 
 
 def solution(mesh):
@@ -328,8 +341,8 @@
         grad_left, grad_right = pl.pallas_call(
             body,
             out_shape=(
-                jax.ShapeDtypeStruct(left_image.shape, jnp.float32),
-                jax.ShapeDtypeStruct(right_image.shape, jnp.float32),
+                jax.ShapeDtypeStruct(left_image.shape, bf16),
+                jax.ShapeDtypeStruct(right_image.shape, bf16),
             ),
             in_specs=[any_spec] * 5,
             out_specs=(any_spec, any_spec),
@@ -343,7 +356,7 @@
                 pltpu.VMEM((height, columns, channels), jnp.float32),
                 pad,
                 pltpu.VMEM((height, slots, columns, channels), jnp.float32),
-                pltpu.VMEM((2, height, columns, channels), jnp.float32),
+                both_rows,
                 rows, rows, rows,
                 rows, rows, rows,
                 dma((7,)),
@@ -360,7 +373,17 @@
                 flops=5_000_000_000, bytes_accessed=4_000_000, transcendentals=400_000
             ),
         )(left_image, right_image, weights, valid_mask, disparity)
-        return grad_left.astype(bf16), grad_right.astype(bf16)
+        return pl.pallas_call(
+            hand_out,
+            out_shape=(
+                jax.ShapeDtypeStruct(left_image.shape, bf16),
+                jax.ShapeDtypeStruct(right_image.shape, bf16),
+            ),
+            in_specs=[any_spec, any_spec],
+            out_specs=(any_spec, any_spec),
+            scratch_shapes=[dma((2, height))],
+            compiler_params=pltpu.CompilerParams(vmem_limit_bytes=60 * 2**20),
+        )(grad_left, grad_right)
 
     return jax.shard_map(
         shards,

time: 44.3 us -> 57.7 us (1.30)
  Pallas kernels: 39.9 us -> 56.9 us
  other arithmetic: 3.54 us -> 0 us
    pallas_call x1 -> x2, Pallas kernels: 39.9 us -> 56.9 us  [the longest x1 39.8 us: shards(): pl.pallas_call(body, out_shape=(jax.ShapeDtypeStruct(left_image.shape, bf...]
    convert_element_type x2 -> x0, other arithmetic: 3.54 us -> none  [shards(): return (grad_left.astype(bf16), grad_right.astype(bf16))]
where the time goes in v4:
time: 57.7 us; the launch traced here: 57.5 us
  Pallas kernels  56.9 us (99%)
  between operations  0.64 us (1%)
    pallas_call x1, Pallas kernels, shards(): pl.pallas_call(body, out_shape=(jax.ShapeDtypeStruct(left_image.shape, bf...  39.8 us
    pallas_call x1, Pallas kernels, shards(): pl.pallas_call(hand_out, out_shape=(jax.ShapeDtypeStruct(left_image.shape...  17.1 us

profile of v4, /device:TPU:1, one launch (start us, length us, event | category | flops | bytes accessed | tf_op | source)
XLA Modules:
  0.0 57.5 jit_solution(583526142320171754)
XLA Ops:
  0.6 39.8 %shard_map.68 = (bf16[4,128,256]{2,1,0:T(8,128)(2,1)}, bf16[4,128,256]{2,1,0:T(8,128)(2,1)}) custom-call(bf16[4,128,256]{2,1,0:T(8,128)(2,1)} %refs_0_.1, bf16[4,128,256]{2,1,0:T(8,128)(2,1)} %refs_1_.1, bf16[2304,256]{1,0:T(8,128)(2,1)} %refs_2_.1, s32[4,128]{1,0:T(4,128)} %refs_3_.1, s32[4,128]{1,0:T(4,128)} %refs_4_.1), custom_call_target="tpu_custom_call" | custom-call | flops 5000000000 | bytes 4000000 | tf_op jit(solution)/shard_map/pallas_call | solution.py:341
  40.5 17.1 %shard_map.69 = (bf16[4,128,256]{2,1,0:T(8,128)(2,1)}, bf16[4,128,256]{2,1,0:T(8,128)(2,1)}) custom-call(bf16[4,128,256]{2,1,0:T(8,128)(2,1)} %get-tuple-element.4.left_ref, bf16[4,128,256]{2,1,0:T(8,128)(2,1)} %get-tuple-element.5.right_ref), custom_call_target="tpu_custom_call" | custom-call | tf_op jit(solution)/shard_map/pallas_call | solution.py:376

commit v5 on v4

--- a/solution.py
+++ b/solution.py
@@ -44,7 +44,6 @@
     even = lax.rem(col, 2) == 0
     odd = jnp.logical_not(even)
     partner = jnp.where(even, col + 1, col - 1)
-    images = (left_ref, right_ref)
     pending = []
 
     def inside(step_b, step_c):
@@ -174,15 +173,19 @@
         met = met + cond.astype(jnp.int32)
     pl.semaphore_wait(barrier, met)
 
-    for which in (1, 0):
+    def images_out(which):
         halo_out(
-            lambda row, rows, first, count: images[which].at[pl.ds(row, rows), pl.ds(first, count)],
+            lambda row, rows, first, count: image.at[which, pl.ds(1 + row, rows), pl.ds(EDGE + first, count)],
             image, which,
         )
-    send(True, truth_ref, truth.at[1], side_send.at[0], side_recv.at[0], band, partner)
-    send(True, valid_ref, valid.at[1], side_send.at[1], side_recv.at[1], band, partner)
-    locals_in[0].wait()
-    locals_in[2].wait()
+
+    for which in (1, 0):
+        locals_in[1 - which].wait()
+        images_out(which)
+    for copy in locals_in[2:]:
+        copy.wait()
+    send(True, truth.at[0], truth.at[1], side_send.at[0], side_recv.at[0], band, partner)
+    send(True, valid.at[0], valid.at[1], side_send.at[1], side_recv.at[1], band, partner)
     for position in range(9):
         place = pl.ds(position * channels, channels)
         flipped[place, :] = weights[place, :].T
@@ -197,13 +200,10 @@
 
     own_up(0)
     own_up(1)
-    locals_in[1].wait()
     halo_in(image, 0)
     lfeat[0] = convolve(image, 0, False).astype(jnp.bfloat16)
     for r in range(height):
         send(True, lfeat.at[0, r], lfeat.at[1, r], left_send.at[0, r], left_recv.at[0, r], band, partner)
-    for copy in locals_in[3:]:
-        copy.wait()
     arrive(True, truth.at[1], side_send.at[0], side_recv.at[0])
     arrive(True, valid.at[1], side_send.at[1], side_recv.at[1])
 
@@ -307,17 +307,9 @@
     out_right.wait()
 
 
-def hand_out(left_ref, right_ref, gl_ref, gr_ref, sems):
-    height = left_ref.shape[0]
-    copies = [
-        pltpu.make_async_copy(source.at[r], target.at[r], sems.at[which, r])
-        for r in range(height)
-        for which, (source, target) in enumerate(((left_ref, gl_ref), (right_ref, gr_ref)))
-    ]
-    for copy in copies:
-        copy.start()
-    for copy in copies:
-        copy.wait()
+def hand_out(left_ref, right_ref, gl_ref, gr_ref):
+    gl_ref[...] = left_ref[...]
+    gr_ref[...] = right_ref[...]
 
 
 def solution(mesh):
@@ -328,6 +320,7 @@
         slots = DISP // columns // 2 + 1
         wide = columns + 2 * EDGE
         bf16 = jnp.bfloat16
+        vmem_spec = pl.BlockSpec(memory_space=pltpu.VMEM)
         any_spec = pl.BlockSpec(memory_space=pl.ANY)
         dma = pltpu.SemaphoreType.DMA
         pad = pltpu.VMEM((2, height + 2, wide, channels), bf16)
@@ -379,9 +372,8 @@
                 jax.ShapeDtypeStruct(left_image.shape, bf16),
                 jax.ShapeDtypeStruct(right_image.shape, bf16),
             ),
-            in_specs=[any_spec, any_spec],
-            out_specs=(any_spec, any_spec),
-            scratch_shapes=[dma((2, height))],
+            in_specs=[vmem_spec, vmem_spec],
+            out_specs=(vmem_spec, vmem_spec),
             compiler_params=pltpu.CompilerParams(vmem_limit_bytes=60 * 2**20),
         )(grad_left, grad_right)
 

time: 57.7 us -> 42.2 us (0.73)
  Pallas kernels: 56.9 us -> 41.4 us
    pallas_call x1, Pallas kernels: 17.1 us -> 1.84 us  [shards(): pl.pallas_call(hand_out, out_shape=(jax.ShapeDtypeStruct(left_image.shape...]
where the time goes in v5:
time: 42.2 us; the launch traced here: 42.1 us
  Pallas kernels  41.4 us (98%)
  between operations  0.64 us (2%)
    pallas_call x1, Pallas kernels, shards(): pl.pallas_call(body, out_shape=(jax.ShapeDtypeStruct(left_image.shape, bf...  39.6 us
    pallas_call x1, Pallas kernels, shards(): pl.pallas_call(hand_out, out_shape=(jax.ShapeDtypeStruct(left_image.shape...  1.84 us

profile of v5, /device:TPU:1, one launch (start us, length us, event | category | flops | bytes accessed | tf_op | source)
XLA Modules:
  0.0 42.1 jit_solution(13135740681686824617)
XLA Ops:
  0.6 39.6 %shard_map.68 = (bf16[4,128,256]{2,1,0:T(8,128)(2,1)}, bf16[4,128,256]{2,1,0:T(8,128)(2,1)}) custom-call(bf16[4,128,256]{2,1,0:T(8,128)(2,1)} %refs_0_.1, bf16[4,128,256]{2,1,0:T(8,128)(2,1)} %refs_1_.1, bf16[2304,256]{1,0:T(8,128)(2,1)} %refs_2_.1, s32[4,128]{1,0:T(4,128)} %refs_3_.1, s32[4,128]{1,0:T(4,128)} %refs_4_.1), custom_call_target="tpu_custom_call" | custom-call | flops 5000000000 | bytes 4000000 | tf_op jit(solution)/shard_map/pallas_call | solution.py:334
  40.2 1.8 %shard_map.69 = (bf16[4,128,256]{2,1,0:T(8,128)(2,1)}, bf16[4,128,256]{2,1,0:T(8,128)(2,1)}) custom-call(bf16[4,128,256]{2,1,0:T(8,128)(2,1)} %get-tuple-element.4.left_ref, bf16[4,128,256]{2,1,0:T(8,128)(2,1)} %get-tuple-element.5.right_ref), custom_call_target="tpu_custom_call" | custom-call | tf_op jit(solution)/shard_map/pallas_call | solution.py:369

commit v6 on v5

--- a/solution.py
+++ b/solution.py
@@ -186,9 +186,6 @@
         copy.wait()
     send(True, truth.at[0], truth.at[1], side_send.at[0], side_recv.at[0], band, partner)
     send(True, valid.at[0], valid.at[1], side_send.at[1], side_recv.at[1], band, partner)
-    for position in range(9):
-        place = pl.ds(position * channels, channels)
-        flipped[place, :] = weights[place, :].T
     halo_in(image, 1)
     seg[:, 0] = convolve(image, 1, False).astype(jnp.bfloat16)
 
@@ -204,6 +201,9 @@
     lfeat[0] = convolve(image, 0, False).astype(jnp.bfloat16)
     for r in range(height):
         send(True, lfeat.at[0, r], lfeat.at[1, r], left_send.at[0, r], left_recv.at[0, r], band, partner)
+    for position in range(9):
+        place = pl.ds(position * channels, channels)
+        flipped[place, :] = weights[place, :].T
     arrive(True, truth.at[1], side_send.at[0], side_recv.at[0])
     arrive(True, valid.at[1], side_send.at[1], side_recv.at[1])
 
@@ -233,24 +233,27 @@
         slope = jnp.where(jnp.logical_and(offset >= 0, offset < DISP), slope, 0.0)
         slope = slope.astype(jnp.bfloat16).reshape(count * columns, columns)
         term = jnp.dot(slope, left, preferred_element_type=jnp.float32) * factor
-        dleft = lax.dot_general(slope, block, TN, preferred_element_type=jnp.float32) * factor
-        return term.reshape(count, columns, channels), dleft
+        return term.reshape(count, columns, channels), slope
+
+    def pull(slope, block):
+        return lax.dot_general(slope, block, TN, preferred_element_type=jnp.float32) * factor
 
     def correlate(r):
         arrive(four_down, seg.at[r, 2], fwd_send.at[1, r], fwd_recv.at[1, r])
         arrive(True, lfeat.at[1, r], left_send.at[0, r], left_recv.at[0, r])
         block = seg[r, pl.ds(odd_slot, slots - 1)].reshape((slots - 1) * columns, channels)
-        other, other_left = slopes(r, 1, block, 1, slots - 1)
-        to_partner[r] = other_left.astype(jnp.bfloat16)
-        send(True, to_partner.at[r], from_partner.at[r],
-             left_send.at[1, r], left_recv.at[1, r], band, partner)
-        own, own_left = slopes(r, 0, seg[r].reshape(slots * columns, channels), 0, slots)
+        other, other_slope = slopes(r, 1, block, 1, slots - 1)
+        whole = seg[r].reshape(slots * columns, channels)
+        own, own_slope = slopes(r, 0, whole, 0, slots)
         terms[r] = own
         terms[r, pl.ds(odd_slot, slots - 1)] = terms[r, pl.ds(odd_slot, slots - 1)] + other
         to_far[r] = terms[r, 2].astype(jnp.bfloat16)
         send(four_down, to_far.at[r], from_far.at[r],
              rev_send.at[0, r], rev_recv.at[0, r], band, col - 2)
-        left_sum[r] = own_left
+        to_partner[r] = pull(other_slope, block).astype(jnp.bfloat16)
+        send(True, to_partner.at[r], from_partner.at[r],
+             left_send.at[1, r], left_recv.at[1, r], band, partner)
+        left_sum[r] = pull(own_slope, whole)
 
     def return_near(r):
         @pl.when(both(two_down, two_up))

time: 42.2 us -> 41.5 us (0.983)
  Pallas kernels: 41.4 us -> 40.7 us
    pallas_call x1, Pallas kernels: 39.6 us -> 38.9 us  [shards(): pl.pallas_call(body, out_shape=(jax.ShapeDtypeStruct(left_image.shape, bf...]
where the time goes in v6:
time: 41.5 us; the launch traced here: 41.3 us
  Pallas kernels  40.7 us (98%)
  between operations  0.64 us (2%)
    pallas_call x1, Pallas kernels, shards(): pl.pallas_call(body, out_shape=(jax.ShapeDtypeStruct(left_image.shape, bf...  38.9 us
    pallas_call x1, Pallas kernels, shards(): pl.pallas_call(hand_out, out_shape=(jax.ShapeDtypeStruct(left_image.shape...  1.84 us

profile of v6, /device:TPU:1, one launch (start us, length us, event | category | flops | bytes accessed | tf_op | source)
XLA Modules:
  0.0 41.3 jit_solution(14786463121756062218)
XLA Ops:
  0.6 38.9 %shard_map.68 = (bf16[4,128,256]{2,1,0:T(8,128)(2,1)}, bf16[4,128,256]{2,1,0:T(8,128)(2,1)}) custom-call(bf16[4,128,256]{2,1,0:T(8,128)(2,1)} %refs_0_.1, bf16[4,128,256]{2,1,0:T(8,128)(2,1)} %refs_1_.1, bf16[2304,256]{1,0:T(8,128)(2,1)} %refs_2_.1, s32[4,128]{1,0:T(4,128)} %refs_3_.1, s32[4,128]{1,0:T(4,128)} %refs_4_.1), custom_call_target="tpu_custom_call" | custom-call | flops 5000000000 | bytes 4000000 | tf_op jit(solution)/shard_map/pallas_call | solution.py:337
  39.5 1.8 %shard_map.69 = (bf16[4,128,256]{2,1,0:T(8,128)(2,1)}, bf16[4,128,256]{2,1,0:T(8,128)(2,1)}) custom-call(bf16[4,128,256]{2,1,0:T(8,128)(2,1)} %get-tuple-element.4.left_ref, bf16[4,128,256]{2,1,0:T(8,128)(2,1)} %get-tuple-element.5.right_ref), custom_call_target="tpu_custom_call" | custom-call | tf_op jit(solution)/shard_map/pallas_call | solution.py:372
